TPU v7x, 32 devices: a whole 2x2x4 slice. The times are simulated.
32 devices in a mesh: dp: 16 (over z, y, x), opt: 2 (over core).
Axes of the slice: x: 2, y: 2, z: 4, core: 2. Of those that a mesh axis runs over, the one named last changes fastest.
Arguments:
- tokens: bfloat16 [16384, 384], P('dp'), may hold values from -6 to 6
- lengths: int32 [16, 16], P('dp'), may hold values from 1 to 128, 1024 in all within a row
- query_index: int32 [128], P('dp'), may hold values from 0 to 15
- doc_index: int32 [128], P('dp'), may hold values from 0 to 15
- targets: int32 [128], P('dp'), may hold values from 0 to 127
- weights: float32 [384, 4608], P('opt')
- first_moment: float32 [384, 4608], P('opt'), may hold values from -1.1920929e-06 to 1.1920929e-06
- second_moment: float32 [384, 4608], P('opt'), may hold values from 5.749459e-15 to 9.1878606e-14
- vectors: float32 [12, 384], P('opt')
- vec_first: float32 [12, 384], P('opt'), may hold values from -4.7683716e-06 to 4.7683716e-06
- vec_second: float32 [12, 384], P('opt'), may hold values from 9.1878606e-14 to 1.4655484e-12
Outputs:
- grad_norm: float32 [], replicated
- input_grad: bfloat16 [16384, 384], P('dp')
- new_weights: float32 [384, 4608], P('opt')
- new_first: float32 [384, 4608], P('opt')
- new_second: float32 [384, 4608], P('opt')
- weight_copy: bfloat16 [384, 4608], P('opt')
- new_vectors: float32 [12, 384], P('opt')
- new_vec_first: float32 [12, 384], P('opt')
- new_vec_second: float32 [12, 384], P('opt')
Inputs may be any that keep to these rules, and one draw needn't show every extreme that they name: `query_index`: row r of the device's rows and segment s in it are named r * 16 + s. `doc_index`: numbered as query_index. `targets`: documents are numbered device by device along dp, in pair order. Each row's lengths sum to 1024.
All inputs are finite; a program needn't handle non-finite values.
Results may differ from a plain program's by a relative error of at most 0.012.
Values may be sent and summed in bfloat16 or wider, within the bound.
No kernel may reach another device: no remote copies, remote signals or barrier semaphores. Data moves between devices by JAX's collectives and lax.ppermute only.
A program may use at most 192 MiB of HBM per device.

v0:
```python
import functools

import jax
import jax.numpy as jnp
from jax import lax
from jax.experimental import pallas as pl
from jax.experimental.pallas import tpu as pltpu
from jax.sharding import PartitionSpec as P

D = 384
HEADS = 12
HD = 32
FF = 1536
SEQ = 1024
SEGS = 16
PAIRS = 8
STEP = 10

WIN = 576
OFF = SEQ - WIN
PAD = 640
BLOCK = 128
BANDS = tuple((q, max(0, q - 128), min(WIN, q + 256)) for q in range(0, WIN, BLOCK))
BAND_ROWS = tuple(sum(b[2] - b[1] for b in BANDS[:i]) for i in range(len(BANDS) + 1))
ROWS = 64
WIDE_ROWS = 192
LOG2E = 1.4426950408889634

LN_EPS = 1e-06
POOL_EPS = 1e-06
SCORE_SCALE = 50.0
CLIP_NORM = 0.001
BETA_ONE = 0.9
BETA_TWO = 0.98
ADAM_EPS = 1e-08
LEARN_RATE = 0.05
VECTOR_RATE = 0.3
DECAY_RATE = 0.01
NEG_BIG = -1e30
HALF = D // 2
CHUNK = HALF // 4
EXP2_SCALE = HD ** (-0.5) * 1.4426950408889634

F32 = jnp.float32
BF16 = jnp.bfloat16
VMEM = pl.BlockSpec(memory_space=pltpu.VMEM)
SMEM = pl.BlockSpec(memory_space=pltpu.SMEM)
ANY = pl.BlockSpec(memory_space=pl.ANY)


def nn(a, b):
    return jnp.dot(a, b, preferred_element_type=F32)


def nt(a, b):
    return lax.dot_general(a, b, (((1,), (1,)), ((), ())), preferred_element_type=F32)


def tn(a, b):
    return lax.dot_general(a, b, (((0,), (0,)), ((), ())), preferred_element_type=F32)


def exact(a, b, dims):
    return lax.dot_general(
        a, b, (dims, ((), ())), precision=lax.Precision.HIGHEST, preferred_element_type=F32
    )


def iota(shape, axis):
    return lax.broadcasted_iota(jnp.int32, shape, axis)


def low_pair(value):
    high = value.astype(BF16)
    return high, (value - high.astype(F32)).astype(BF16)


def aligned(start, size, unit):
    return pl.ds(pl.multiple_of(start, unit), size)


def assemble(dst, own, other, opt):
    dst[aligned(HALF * opt, HALF, 64), :] = own[0:HALF, :]
    dst[aligned(HALF * (1 - opt), HALF, 64), :] = other[0:HALF, :]


class Place:
    def __getitem__(self, i):
        if i == 0:
            return lax.axis_index("opt")
        me = lax.axis_index("dp")
        return (me & 3, me, (me >> 2) & 3)[i - 1]


def call(kernel, ins, outs, scratch=(), micros=5, name=None, vmem=12, after=()):
    if ins[0][1] is None:
        kernel = functools.partial(kernel, Place())
        ins = ins[1:]
    specs = [SMEM if s else VMEM for s, _ in ins] + [ANY] * len(after)
    count = len(ins)

    def body(*refs):
        kernel(*refs[:count], *refs[count + len(after) :])

    shapes = [jax.ShapeDtypeStruct(s, d) for s, d in outs]
    moved = sum(a.size * a.dtype.itemsize for _, a in ins)
    moved += sum(s.size * s.dtype.itemsize for s in shapes)
    return pl.pallas_call(
        body,
        out_shape=shapes,
        in_specs=specs,
        out_specs=[VMEM] * len(shapes),
        scratch_shapes=list(scratch),
        compiler_params=pltpu.CompilerParams(vmem_limit_bytes=vmem << 20),
        cost_estimate=pl.CostEstimate(
            flops=micros * 1100000000, bytes_accessed=moved, transcendentals=0
        ),
        name=name,
    )(*[a for _, a in ins], *after)


def head_stack(rows):
    lane_head = iota(rows.shape, 1) // HD
    zero = jnp.zeros_like(rows)
    return jnp.concatenate([jnp.where(lane_head == j, rows, zero) for j in range(4)], axis=0)


def attend_kernel(
    place, scalars, tokens, w_own, w_other, v_own, v_other,
    proj, att, lse, segc, segr, ownc, ownr, wanted, marks, vec, wfull, bias, vt,
):
    opt = place[0]
    assemble(wfull, w_own, w_other, opt)
    mine = v_own[...].astype(BF16).astype(F32)
    others = v_other[...].astype(BF16).astype(F32)
    first = opt == 0
    vec[0:6, :] = jnp.where(first, mine, others)
    vec[6:12, :] = jnp.where(first, others, mine)
    vec[12:16, :] = jnp.zeros((4, D), F32)

    position = iota((8, PAD), 1) + OFF * opt
    segment = jnp.zeros((8, PAD), jnp.int32)
    bound = jnp.int32(0)
    low_count = jnp.int32(0)
    for s in range(SEGS):
        bound = bound + scalars[s]
        segment = segment + (position >= bound).astype(jnp.int32)
        low_count = low_count + (bound <= WIN).astype(jnp.int32)
    mine = (segment < low_count).astype(jnp.int32) == (opt == 0).astype(jnp.int32)
    owned = jnp.where(mine, segment, -1)
    segr[...] = segment
    ownr[...] = owned
    for value, out in ((segment, segc), (owned, ownc)):
        value = value.astype(F32)
        for t in range(PAD // 128):
            rows = min(128, WIN - 128 * t)
            turned = jnp.broadcast_to(value[0:1, 128 * t : 128 * t + 128], (128, 128)).T
            out[128 * t : 128 * t + rows, :] = turned[0:rows].astype(jnp.int32)
    row, col = iota((2 * PAIRS, 128), 0), iota((2 * PAIRS, 128), 1)
    by_row = jnp.zeros((2 * PAIRS, 128), jnp.int32)
    by_col = jnp.zeros((2 * PAIRS, 128), jnp.int32)
    mark = jnp.zeros((2 * PAIRS, 128), jnp.int32)
    for j in range(PAIRS):
        mark = jnp.where(row == j, scalars[SEGS + 2 * PAIRS + j], mark)
        for at in (j, PAIRS + j):
            by_row = jnp.where(row == at, scalars[SEGS + at], by_row)
            by_col = jnp.where(col == at, scalars[SEGS + at], by_col)
    wanted[0] = by_row
    wanted[1] = by_col
    marks[...] = jnp.where(col < 64, mark >> 5, mark & 31).astype(F32).astype(BF16)
    for i, (q0, k0, k1) in enumerate(BANDS):
        bias[BAND_ROWS[i] : BAND_ROWS[i + 1], :] = jnp.where(
            segc[k0:k1, :] == segr[0:1, q0 : q0 + BLOCK], 0.0, NEG_BIG
        )

    x = tokens[aligned(OFF * opt, WIN, 64), :]
    bias_row = jnp.concatenate([vec[0:1, :], jnp.zeros((1, D), F32), vec[1:2, :]], axis=1)
    for first in range(0, 3 * D, 512):
        cols = slice(first, min(first + 512, 3 * D))
        proj[0:WIN, cols] = (nn(x, wfull[:, cols]) + bias_row[:, cols]).astype(BF16)
    proj[WIN:PAD, :] = jnp.zeros((PAD - WIN, 3 * D), BF16)

    def group(g, carry):
        def lanes(part):
            return aligned(part * D + 128 * g, 128, 128)

        for t in range(PAD // 128):
            vt[:, 128 * t : 128 * t + 128] = (
                proj[128 * t : 128 * t + 128, lanes(2)].astype(F32).T.astype(BF16)
            )
        def scores(i):
            q0, k0, k1 = BANDS[i]
            return nt(proj[k0:k1, lanes(1)], head_stack(proj[q0 : q0 + BLOCK, lanes(0)]))

        coming = scores(0)
        for i, (q0, k0, k1) in enumerate(BANDS):
            st = coming
            if i + 1 < len(BANDS):
                coming = scores(i + 1)
            outs, probs, totals = [], [], []
            for j in range(4):
                t = (
                    st[:, j * BLOCK : (j + 1) * BLOCK] * EXP2_SCALE
                    + bias[BAND_ROWS[i] : BAND_ROWS[i + 1], :]
                )
                peak = jnp.max(t, axis=0, keepdims=True)
                powers = jnp.exp2(t - peak)
                total = jnp.sum(powers, axis=0, keepdims=True)
                lse[g, j : j + 1, q0 : q0 + BLOCK] = peak + jnp.log2(total)
                probs.append(powers.astype(BF16))
                totals.append(1.0 / total)
                if j % 2 == 1:
                    o = nn(vt[(j - 1) * HD : (j + 1) * HD, k0:k1], jnp.concatenate(probs[-2:], axis=1))
                    outs.append(o[0:HD, 0:BLOCK] * totals[-2])
                    outs.append(o[HD : 2 * HD, BLOCK : 2 * BLOCK] * totals[-1])
            rows = min(BLOCK, WIN - q0)
            att[q0 : q0 + rows, aligned(128 * g, 128, 128)] = (
                jnp.concatenate(outs, axis=0).T[0:rows].astype(BF16)
            )
        return carry

    lax.fori_loop(0, 3, group, 0)


def attend(place, scalars, arrays):
    return call(
        attend_kernel,
        [(1, place), (1, scalars)] + [(0, a) for a in arrays],
        [
            ((PAD, 3 * D), BF16),
            ((WIN, D), BF16),
            ((3, 4, PAD), F32),
            ((WIN, 128), jnp.int32),
            ((8, PAD), jnp.int32),
            ((WIN, 128), jnp.int32),
            ((8, PAD), jnp.int32),
            ((2, 2 * PAIRS, 128), jnp.int32),
            ((2 * PAIRS, 128), BF16),
            ((16, D), F32),
            ((D, 3 * D), BF16),
        ],
        [
            pltpu.VMEM((BAND_ROWS[-1], 128), F32),
            pltpu.VMEM((128, PAD), BF16),
        ],
        micros=8,
        name="attend",
    )


def cast_kernel(weights, wq, wo, wu, wd, buffer, sems):
    spans = [(wq, 3 * D), (wo, D), (wu, FF), (wd, FF)]
    copies = [
        pltpu.make_async_copy(
            weights.at[:, i * D : (i + 1) * D], buffer.at[:, i * D : (i + 1) * D], sems.at[i]
        )
        for i in range(12)
    ]
    for copy in copies:
        copy.start()
    at = 0
    for out, width in spans:
        for part in range(width // D):
            copies[at].wait()
            out[:, part * D : (part + 1) * D] = buffer[:, at * D : (at + 1) * D].astype(BF16)
            at += 1


def cast(weights):
    return pl.pallas_call(
        cast_kernel,
        out_shape=[jax.ShapeDtypeStruct((HALF, c), BF16) for c in (3 * D, D, FF, FF)],
        in_specs=[ANY],
        out_specs=[VMEM] * 4,
        scratch_shapes=[pltpu.VMEM(weights.shape, F32), pltpu.SemaphoreType.DMA((12,))],
        compiler_params=pltpu.CompilerParams(vmem_limit_bytes=52 << 20),
        name="cast",
    )(weights)


def bias_of(vec, c):
    first, last = 256 * c, 256 * c + 256
    parts = []
    while first < last:
        row, col = divmod(first, D)
        size = min(D - col, last - first)
        parts.append(vec[3 + row : 4 + row, col : col + size])
        first += size
    return parts[0] if len(parts) == 1 else jnp.concatenate(parts, axis=1)


def mlp_kernel(
    place, wanted, att, tokens, ownr, vec, wo_own, wo_other, wu_own, wu_other,
    wd_own, wd_other, xhat1, inv1, hlow, act, up_proj, xhat2, inv2, unit, uscale, wo, wu, wd,
    ench, encl,
):
    opt = place[0]
    assemble(wo, wo_own, wo_other, opt)
    assemble(wu, wu_own, wu_other, opt)
    assemble(wd, wd_own, wd_other, opt)

    def norm(v):
        centred = v - jnp.mean(v, axis=1, keepdims=True)
        inverse = lax.rsqrt(jnp.mean(centred * centred, axis=1, keepdims=True) + LN_EPS)
        return centred * inverse, inverse

    def block(i, carry):
        r = aligned(i * WIDE_ROWS, WIDE_ROWS, 64)
        x = tokens[aligned(OFF * opt + i * WIDE_ROWS, WIDE_ROWS, 64), :].astype(F32)
        normed, inverse = norm(nn(att[r, :], wo[...]) + vec[2:3, :] + x)
        xhat1[r, :] = normed
        inv1[r, :] = jnp.broadcast_to(inverse, (WIDE_ROWS, 128))
        h = normed * vec[8:9, :] + vec[9:10, :]
        low = h.astype(BF16)
        hlow[r, :] = low
        coming = nn(low, wu[:, 0:256])
        for c in range(6):
            cols = slice(c * 256, (c + 1) * 256)
            u = coming + bias_of(vec, c)
            if c < 5:
                coming = nn(low, wu[:, (c + 1) * 256 : (c + 2) * 256])
            up_proj[r, cols] = u
            half = lax.erf(u * 0.7071067811865476) * 0.5 + 0.5
            act[r, cols] = (u * half).astype(BF16)
        normed, inverse = norm(nt(act[r, :], wd[...]) + vec[7:8, :] + h)
        xhat2[r, :] = normed
        inv2[r, :] = jnp.broadcast_to(inverse, (WIDE_ROWS, 128))
        high, rest = low_pair(normed * vec[10:11, :] + vec[11:12, :])
        ench[r, :] = high
        encl[r, :] = rest
        return carry

    lax.fori_loop(0, WIN // WIDE_ROWS, block, 0)

    onehot = jnp.where(wanted[0, :, 0:1] == ownr[0:1, 0:WIN], 1.0, 0.0)
    count = jnp.maximum(jnp.sum(onehot, axis=1, keepdims=True), 1.0)
    hot = onehot.astype(BF16)
    pooled = (nn(hot, ench[...]) + nn(hot, encl[...])) / count
    inverse_len = lax.rsqrt(jnp.sum(pooled * pooled, axis=1, keepdims=True) + POOL_EPS)
    unit[...] = pooled * inverse_len
    uscale[...] = jnp.broadcast_to(inverse_len / count, (2 * PAIRS, 128))


def slope_kernel(up_proj, out):
    def block(i, carry):
        r = aligned(i * 16, 16, 16)
        u = up_proj[r, :]
        half = lax.erf(u * 0.7071067811865476) * 0.5 + 0.5
        out[r, :] = half + u * jnp.exp2(u * u * (-0.5 * LOG2E)) * 0.3989422804014327
        return carry

    lax.fori_loop(0, WIN // 16, block, 0)


def slope_of(up_proj, after):
    return call(slope_kernel, [(0, up_proj)], [(up_proj.shape, F32)], name="slope", vmem=4, after=after)[0]


def mlp(place, wanted, att, tokens, ownr, vec, halves):
    return call(
        mlp_kernel,
        [(1, place), (0, wanted), (0, att), (0, tokens), (0, ownr), (0, vec)]
        + [(0, h) for h in halves],
        [
            ((WIN, D), F32),
            ((WIN, 128), F32),
            ((WIN, D), BF16),
            ((WIN, FF), BF16),
            ((WIN, FF), F32),
            ((WIN, D), F32),
            ((WIN, 128), F32),
            ((2 * PAIRS, D), F32),
            ((2 * PAIRS, 128), F32),
            ((D, D), BF16),
            ((D, FF), BF16),
            ((D, FF), BF16),
        ],
        [
            pltpu.VMEM((WIN, D), BF16),
            pltpu.VMEM((WIN, D), BF16),
        ],
        micros=10,
        name="mlp",
    )


def split_rows(grad, keep, send, place, *at):
    opt = place[0]
    for c in range(4):
        index = (c ^ place[1],) + at
        keep[index] = grad[aligned(HALF * opt + CHUNK * c, CHUNK, 16), :].astype(BF16)
        send[index] = grad[aligned(HALF * (1 - opt) + CHUNK * c, CHUNK, 16), :].astype(BF16)


def column_sums(value):
    return jnp.sum(value.reshape(-1, 8, D), axis=0)


def norm_backward(grad_at, normed_ref, inverse_ref, gain, out, low_out, sums, at, step=ROWS):
    def block(i, carry):
        scale_sum, shift_sum, bias_sum = carry
        r = aligned(i * step, step, 64)
        g = grad_at(r)
        normed = normed_ref[r, :]
        scaled = g * gain
        inner = (
            scaled
            - jnp.mean(scaled, axis=1, keepdims=True)
            - normed * jnp.mean(scaled * normed, axis=1, keepdims=True)
        ) * inverse_ref[r, 0:1]
        out[r, :] = inner
        low_out[r, :] = inner.astype(BF16)
        return (
            scale_sum + column_sums(g * normed),
            shift_sum + column_sums(g),
            bias_sum + column_sums(inner),
        )

    zero = jnp.zeros((8, D), F32)
    scale_sum, shift_sum, bias_sum = lax.fori_loop(0, WIN // step, block, (zero, zero, zero))
    sums[at : at + 1, :] = jnp.sum(bias_sum, axis=0, keepdims=True)
    sums[at + 1 : at + 2, :] = jnp.sum(scale_sum, axis=0, keepdims=True)
    sums[at + 2 : at + 3, :] = jnp.sum(shift_sum, axis=0, keepdims=True)


def down_kernel(
    place, count, order, wanted, units, ownc, uscale, xhat2, inv2, act, vec, *rest
):
    pieces, (dsec, dlow, keep, send, sums, queries, docs, marks, grad) = rest[:-9], rest[-9:]
    me = place[2]
    per = pieces[0].shape[0]
    for p, piece in enumerate(pieces):
        for j in range(per):
            at = order[p * per + j]
            r = slice(at * PAIRS, (at + 1) * PAIRS)
            both = piece[j].astype(F32)
            queries[r, :] = both[0:PAIRS, 0:D]
            docs[r, :] = both[PAIRS : 2 * PAIRS, 0:D]
            marks[r, :] = both[0:PAIRS, D : D + 128]
    total = count * PAIRS
    q = queries[...].astype(BF16)
    d = docs[...].astype(BF16)
    logits = SCORE_SCALE * nt(q, d)
    peak = jnp.max(logits, axis=1, keepdims=True)
    powers = jnp.exp(logits - peak)
    soft = powers / jnp.sum(powers, axis=1, keepdims=True)
    col = iota((total, total), 1)
    doc_id = ((col // PAIRS) ^ me) * PAIRS + lax.rem(col, PAIRS)
    hit = (marks[:, 0:1] * 32.0 + marks[:, 64:65]).astype(jnp.int32) == doc_id
    d_logits = (soft - jnp.where(hit, 1.0, 0.0)) * (SCORE_SCALE / total)
    high, rest_low = low_pair(d_logits[0:PAIRS, :])
    d_q = nn(high, d) + nn(rest_low, d)
    high, rest_low = low_pair(d_logits[:, 0:128].T[0:PAIRS, :])
    d_d = nn(high, q) + nn(rest_low, q)
    d_units = jnp.concatenate([d_q, d_d], axis=0)
    u = units[...]
    d_pool = uscale[:, 0:1] * (d_units - u * jnp.sum(u * d_units, axis=1, keepdims=True))
    hot = jnp.where(ownc[:, 0 : 2 * PAIRS] == wanted[1, 0:1, 0 : 2 * PAIRS], 1.0, 0.0).astype(BF16)
    high, rest_low = low_pair(d_pool)
    dsec[...] = nn(hot, high) + nn(hot, rest_low)
    norm_backward(lambda r: dsec[r, :], xhat2, inv2, vec[10:11, :], dsec, dlow, sums, 0)
    sums[3:8, :] = jnp.zeros((5, D), F32)
    for c in range(3):
        cols = slice(c * 512, (c + 1) * 512)
        grad[:, cols] = tn(dlow[...], act[:, cols])
    for c in range(4):
        split_rows(grad.at[:, c * D : (c + 1) * D], keep, send, place, c)


def down_backward(count, order, place, wanted, units, ownc, uscale, saved, vec, pieces, after):
    total = count * PAIRS
    return call(
        lambda place, *refs: down_kernel(place, count, order, *refs),
        [(1, place), (0, wanted), (0, units), (0, ownc), (0, uscale)]
        + [(0, s) for s in saved]
        + [(0, vec)]
        + [(0, p) for p in pieces],
        [
            ((WIN, D), F32),
            ((WIN, D), BF16),
            ((4, 4, CHUNK, D), BF16),
            ((4, 4, CHUNK, D), BF16),
            ((8, D), F32),
        ],
        [
            pltpu.VMEM((total, D), F32),
            pltpu.VMEM((total, D), F32),
            pltpu.VMEM((total, 128), F32),
            pltpu.VMEM((D, FF), F32),
        ],
        micros=4,
        name="down_backward",
        after=after,
    )


def up_kernel(place, dlow, slope, hlow, wd, dup, keep, send, sums, grad):
    coming = nn(dlow[...], wd[:, 0:512])
    for c in range(3):
        cols = slice(c * 512, (c + 1) * 512)
        part = (coming * slope[:, cols]).astype(BF16)
        if c < 2:
            coming = nn(dlow[...], wd[:, (c + 1) * 512 : (c + 2) * 512])
        dup[:, cols] = part
        column_sum = jnp.sum(part.astype(F32), axis=0, keepdims=True)
        for j in range(4):
            at = 512 * c + 128 * j
            sums[at // D : at // D + 1, at % D : at % D + 128] = column_sum[:, 128 * j : 128 * j + 128]
        grad[:, cols] = tn(hlow[...], dup[:, cols])
    for c in range(4):
        split_rows(grad.at[:, c * D : (c + 1) * D], keep, send, place, c)


def up_backward(place, dlow, slope, hlow, wd, after):
    return call(
        up_kernel,
        [(1, place)] + [(0, a) for a in (dlow, slope, hlow, wd)],
        [((WIN, FF), BF16), ((4, 4, CHUNK, D), BF16), ((4, 4, CHUNK, D), BF16), ((4, D), F32)],
        [pltpu.VMEM((D, FF), F32)],
        micros=3,
        name="up_backward",
        after=after,
    )


def first_kernel(
    place, dup, dsec, xhat1, inv1, att, vec, wu, wo,
    dfirst, datt, delta, okeep, osend, sums, grad, dlow,
):
    steps = [slice(i, i + WIDE_ROWS) for i in range(0, WIN, WIDE_ROWS)]
    coming = nt(dup[steps[0], :], wu[...])
    gain = vec[8:9, :]
    totals = None
    for i, r in enumerate(steps):
        g = coming + dsec[r, :]
        if i + 1 < len(steps):
            coming = nt(dup[steps[i + 1], :], wu[...])
        normed = xhat1[r, :]
        scaled = g * gain
        inner = (
            scaled
            - jnp.mean(scaled, axis=1, keepdims=True)
            - normed * jnp.mean(scaled * normed, axis=1, keepdims=True)
        ) * inv1[r, 0:1]
        dfirst[r, :] = inner
        dlow[r, :] = inner.astype(BF16)
        new = [column_sums(inner), column_sums(g * normed), column_sums(g)]
        totals = new if totals is None else [a + b for a, b in zip(totals, new)]
    for i, total in enumerate(totals):
        sums[i : i + 1, :] = jnp.sum(total, axis=0, keepdims=True)
    sums[3:8, :] = jnp.zeros((5, D), F32)
    grad[...] = tn(att[...], dlow[...])
    split_rows(grad, okeep, osend, place)
    da = nt(dlow[...], wo[...]).astype(BF16)
    datt[0:WIN, :] = da
    datt[WIN:PAD, :] = jnp.zeros((PAD - WIN, D), BF16)
    high, rest = low_pair(da.astype(F32) * att[...].astype(F32))
    heads = (iota((16, D), 1) // HD == iota((16, D), 0)).astype(F32).astype(BF16)
    delta[:, 0:WIN] = nt(heads, high) + nt(heads, rest)
    delta[:, WIN:PAD] = jnp.zeros((16, PAD - WIN), F32)


def first_backward(place, dup, dsec, xhat1, inv1, att, vec, wu, wo, after):
    return call(
        first_kernel,
        [(1, place)] + [(0, a) for a in (dup, dsec, xhat1, inv1, att, vec, wu, wo)],
        [
            ((WIN, D), F32),
            ((PAD, D), BF16),
            ((16, PAD), F32),
            ((4, CHUNK, D), BF16),
            ((4, CHUNK, D), BF16),
            ((8, D), F32),
        ],
        [
            pltpu.VMEM((D, D), F32),
            pltpu.VMEM((WIN, D), BF16),
        ],
        micros=1,
        name="first_backward",
        after=after,
    )


def heads_kernel(place, g, tokens, proj, datt, lse, delta, segc, segr, *rest):
    rest, (dproj, keep, send, sums, kt, dk, dv, grad, ktmp, stmp) = rest[:-10], rest[-10:]

    def lanes(part):
        return slice(part * D + 128 * g, part * D + 128 * g + 128)

    for t in range(PAD // 128):
        kt[:, 128 * t : 128 * t + 128] = (
            proj[128 * t : 128 * t + 128, lanes(1)].astype(F32).T.astype(BF16)
        )
    dk[...] = jnp.zeros_like(dk)
    dv[...] = jnp.zeros_like(dv)

    def products(i):
        q0, k0, k1 = BANDS[i]
        qs = head_stack(proj[q0 : q0 + BLOCK, lanes(0)])
        gs = head_stack(datt[q0 : q0 + BLOCK, lanes(0)])
        return qs, gs, nt(proj[k0:k1, lanes(1)], qs), nt(proj[k0:k1, lanes(2)], gs)

    coming = products(0)
    for i, (q0, k0, k1) in enumerate(BANDS):
        qs, gs, st, dp = coming
        if i + 1 < len(BANDS):
            coming = products(i + 1)
        same = segc[k0:k1, :] == segr[0:1, q0 : q0 + BLOCK]
        bias = jnp.where(same, 0.0, NEG_BIG)
        probs, d_scores, dq = [], [], []
        for j in range(4):
            cols = slice(j * BLOCK, (j + 1) * BLOCK)
            prob = jnp.exp2(st[:, cols] * EXP2_SCALE + bias - lse[g, j : j + 1, q0 : q0 + BLOCK])
            ds = prob * (dp[:, cols] - delta[4 * g + j : 4 * g + j + 1, q0 : q0 + BLOCK])
            ds = ds.astype(BF16)
            probs.append(prob.astype(BF16))
            d_scores.append(ds)
            if j % 2 == 1:
                part = nn(
                    kt[(j - 1) * HD : (j + 1) * HD, k0:k1], jnp.concatenate(d_scores[-2:], axis=1)
                )
                dq.append(part[0:HD, 0:BLOCK])
                dq.append(part[HD : 2 * HD, BLOCK : 2 * BLOCK])
        dv[k0:k1, :] += nn(jnp.concatenate(probs, axis=1), gs)
        dk[k0:k1, :] += nn(jnp.concatenate(d_scores, axis=1), qs)
        rows = min(BLOCK, WIN - q0)
        dqs = jnp.concatenate(dq, axis=0).T[0:rows] * HD ** (-0.5)
        dproj[q0 : q0 + rows, 0:128] = dqs.astype(BF16)
    dproj[:, 128:256] = (dk[...] * HD ** (-0.5)).astype(BF16)
    dproj[:, 256:384] = dv[...].astype(BF16)
    grad[...] = tn(tokens[aligned(OFF * place[0], WIN, 64), :], dproj[...])
    q_sum = jnp.sum(dproj[:, 0:128].astype(F32), axis=0, keepdims=True)
    v_sum = jnp.sum(dproj[:, 256:384].astype(F32), axis=0, keepdims=True)
    sums[0:1, :] = q_sum
    sums[1:2, :] = v_sum
    sums[2:8, :] = jnp.zeros((6, 128), F32)
    if g < 2:
        split_rows(grad, keep, send, place)
        return
    parts, (dsums, usums, fsums, zero, one) = rest[:6], rest[6:]
    split_rows(grad, ktmp, stmp, place)
    for dst, out_part, blocks in (
        (keep, parts[0], (parts[2], parts[4], ktmp)),
        (send, parts[1], (parts[3], parts[5], stmp)),
    ):
        dst[:, :, 3 * D : 4 * D] = out_part[...]
        for h, part in enumerate(blocks):
            for c in range(3):
                dst[:, :, D * c + 128 * h : D * c + 128 * h + 128] = part[
                    :, :, 128 * c : 128 * c + 128
                ]
    rows = jnp.concatenate(
        [
            jnp.concatenate([zero[0:1], one[0:1], q_sum], axis=1),
            jnp.concatenate([zero[1:2], one[1:2], v_sum], axis=1),
            fsums[0:1, :],
            usums[0:4, :],
            dsums[0:1, :],
            fsums[1:3, :],
            dsums[1:3, :],
            jnp.zeros((4, D), F32),
        ],
        axis=0,
    ).astype(BF16)
    for c in range(4):
        for j in range(3):
            block = rows[:, 128 * j : 128 * j + 128]
            keep[c, 16 * j : 16 * j + 16, 4 * D : 4 * D + 128] = block
            send[c, 16 * j : 16 * j + 16, 4 * D : 4 * D + 128] = block


def heads_backward(g, place, ins, more, after):
    part = ((4, CHUNK, 4 * D + 128 if g == 2 else D), BF16)
    return call(
        lambda place, *refs: heads_kernel(place, g, *refs),
        [(1, place)] + [(0, a) for a in tuple(ins) + tuple(more)],
        [((WIN, D), BF16), part, part, ((8, 128), F32)],
        [
            pltpu.VMEM((128, PAD), BF16),
            pltpu.VMEM((WIN, 128), F32),
            pltpu.VMEM((WIN, 128), F32),
            pltpu.VMEM((D, D), F32),
            pltpu.VMEM((4, CHUNK, D), BF16),
            pltpu.VMEM((4, CHUNK, D), BF16),
        ],
        micros=1,
        name="heads_backward",
        after=after,
    )


def input_kernel(dp0, dp1, dp2, dfirst, wfull, igrad, dproj):
    for g, part in enumerate((dp0, dp1, dp2)):
        for c in range(3):
            dproj[:, c * D + 128 * g : c * D + 128 * g + 128] = part[:, 128 * c : 128 * c + 128]
    igrad[...] = (nt(dproj[...], wfull[...]) + dfirst[...]).astype(BF16)


def input_backward(parts, dfirst, wqkv, after):
    return call(
        input_kernel,
        [(0, a) for a in tuple(parts) + (dfirst, wqkv)],
        [((WIN, D), BF16)],
        [pltpu.VMEM((WIN, 3 * D), BF16)],
        micros=2,
        name="input_backward",
        after=after,
    )[0]


def flips(axis, size, bits):
    return [(i, i ^ bits) for i in range(size)]


def pair(value):
    return swap(value, "opt", 2, 1)


def swap(value, axis, size, bits):
    return lax.ppermute(value, axis, flips(axis, size, bits))


def bit_groups(size):
    bits = size.bit_length() - 1
    return [(s, 1 << min(2, bits - s)) for s in range(0, bits, 2)]


def trades(values, n, shift):
    return [values[0]] + [swap(values[k], "dp", n, k << shift) for k in (1, 2, 3)]


def added(a, b):
    return (a.astype(F32) + b.astype(F32)).astype(BF16)


def core_sum_kernel(keep, other, *outs):
    for r, out in enumerate(outs):
        out[...] = added(keep[r], other[r])


def core_sum(keep, other, after):
    return call(
        core_sum_kernel,
        [(0, keep), (0, other)],
        [(keep.shape[1:], BF16)] * 4,
        name="core_sum",
        vmem=4,
        after=after,
    )


def pair_sum_kernel(bit, keep, other, stay, go):
    for i, r in enumerate((0, 3 - bit)):
        stay[i] = added(keep[r], other[r])
        go[i] = added(keep[r + bit], other[r + bit])


def pair_sum(bit, keep, other, after):
    return call(
        functools.partial(pair_sum_kernel, bit),
        [(0, keep), (0, other)],
        [((2,) + keep.shape[1:], BF16)] * 2,
        name="pair_sum",
        vmem=4,
        after=after,
    )


def wide_step_kernel(down, dother, up, uother, dkeep, dsend, ukeep, usend):
    dkeep[...] = added(down[0], dother[0])
    dsend[...] = added(down[1], dother[1])
    ukeep[...] = added(up[0], uother[0])
    usend[...] = added(up[1], uother[1])


def wide_step(parts, after):
    return call(
        wide_step_kernel,
        [(0, p) for p in parts],
        [((4, CHUNK, D), BF16)] * 4,
        name="wide_step",
        vmem=4,
        after=after,
    )


def total_of(refs, at):
    a, b, c, d = (ref[at].astype(F32) for ref in refs)
    return ((a + b) + (c + d)).astype(BF16)


def wide_plane_kernel(place, down, dother, up, uother, *outs):
    for k, out in enumerate(outs):
        at = place[3] ^ k
        out[0] = added(down[at], dother[at])
        out[1] = added(up[at], uother[at])


def wide_plane_sum(place, parts, after):
    return call(
        wide_plane_kernel,
        [(1, place)] + [(0, p) for p in parts],
        [((2, CHUNK, D), BF16)] * 4,
        name="wide_plane_sum",
        vmem=4,
        after=after,
    )


def low_plane_kernel(a, b, c, d, out):
    out[...] = total_of((a, b, c, d), slice(None))


def low_plane_sum(parts, after=()):
    return call(
        low_plane_kernel,
        [(0, p) for p in parts],
        [(parts[0].shape, BF16)],
        name="low_plane_sum",
        vmem=4,
        after=after,
    )[0]


def low_next_kernel(keep, other, out):
    out[...] = added(keep[...], other[...])


def low_next(keep, other, after=()):
    return call(
        low_next_kernel,
        [(0, keep), (0, other)],
        [(keep.shape, BF16)],
        name="low_next",
        vmem=4,
        after=after,
    )[0]


def low_last_kernel(keep, other, out, vgrad):
    out[...] = added(keep[:, 0 : 4 * D], other[:, 0 : 4 * D])
    vgrad[...] = added(keep[:, 4 * D : 4 * D + 128], other[:, 4 * D : 4 * D + 128])


def low_last(keep, other, after):
    return call(
        low_last_kernel,
        [(0, keep), (0, other)],
        [((CHUNK, 4 * D), BF16), ((CHUNK, 128), BF16)],
        name="low_last",
        vmem=4,
        after=after,
    )


def chain_kernel(*refs):
    ins, out = refs[:-1], refs[-1]
    at = 0
    for ref in ins:
        flat = ref.reshape(-1, CHUNK, D)
        out[at : at + flat.shape[0]] = flat[...]
        at += flat.shape[0]


def chain(parts, after=()):
    count = sum(p.size for p in parts) // (CHUNK * D)
    return call(
        chain_kernel,
        [(0, p) for p in parts],
        [((count, CHUNK, D), BF16)],
        name="chain",
        vmem=4,
        after=after,
    )[0]


def rest_sum(value, n):
    bit = 16
    while bit < n:
        other = swap(value, "dp", n, bit)
        value = (value.astype(F32) + other.astype(F32)).astype(BF16)
        bit *= 2
    return value


def join_kernel(*refs):
    ins, out = refs[:-1], refs[-1]
    for i, ref in enumerate(ins):
        out[i] = ref[...]


def join(parts, after=()):
    return call(
        join_kernel,
        [(0, p) for p in parts],
        [((len(parts),) + parts[0].shape, parts[0].dtype)],
        name="join",
        vmem=4,
        after=after,
    )[0]


def pack_kernel(marks, unit, other, units, packed):
    both = unit[...] + other[...]
    units[...] = both
    packed[:, 0:D] = both.astype(BF16)
    packed[:, D : D + 128] = marks[...]


def pack(marks, unit, other):
    return call(
        pack_kernel,
        [(0, marks), (0, unit), (0, other)],
        [(unit.shape, F32), ((2 * PAIRS, D + 128), BF16)],
        name="pack",
        vmem=4,
    )


def squares_of(parts):
    acc = jnp.zeros((8, D), F32)
    for part in parts:
        flat = part.reshape(-1, CHUNK, part.shape[-1])
        for k in range(flat.shape[0]):
            for c in range(0, part.shape[-1], D):
                v = flat[k, :, c : c + D].astype(F32)
                acc = acc + jnp.sum((v * v).reshape(CHUNK // 8, 8, D), axis=0)
    return acc[:, 0:128] + acc[:, 128:256] + acc[:, 256:384]


def wide_squares_kernel(*refs):
    refs[-1][...] = squares_of(refs[:-1])


def squares_kernel(place, *refs):
    parts, (vgrad, before, out) = refs[:-3], refs[-3:]
    acc = squares_of(parts) + before[...]
    row = iota((16, 128), 0)
    low_row = 6 * place[0]
    mine = (row >= low_row) & (row < low_row + 6)
    for j in range(3):
        v = jnp.where(mine, vgrad[16 * j : 16 * j + 16, :].astype(F32), 0.0)
        v = v * v
        acc = acc + (v[0:8] + v[8:16])
    out[...] = acc


def squares(place, parts, vgrad=None, before=None, after=()):
    ins = [(0, p) for p in parts]
    kernel = wide_squares_kernel
    if before is not None:
        ins = [(1, place)] + ins + [(0, vgrad), (0, before)]
        kernel = squares_kernel
    return call(kernel, ins, [((8, 128), F32)], name="squares", vmem=4, after=after)[0]


def merge_kernel(place, igrad, other, out, flag):
    flag[...] = jnp.zeros((8, 128), F32)

    @pl.when(place[0] == 0)
    def low_core():
        out[0:OFF, :] = igrad[0:OFF, :]
        out[OFF:WIN, :] = added(igrad[OFF:WIN, :], other[0 : WIN - OFF, :])
        out[WIN:SEQ, :] = other[WIN - OFF : WIN, :]

    @pl.when(place[0] != 0)
    def high_core():
        out[0:OFF, :] = other[0:OFF, :]
        out[OFF:WIN, :] = added(other[OFF:WIN, :], igrad[0 : WIN - OFF, :])
        out[WIN:SEQ, :] = igrad[WIN - OFF : WIN, :]


def merge(place, igrad, other, after):
    return call(
        merge_kernel,
        [(1, place), (0, igrad), (0, other)],
        [((SEQ, D), BF16), ((8, 128), F32)],
        name="merge",
        vmem=4,
        after=after,
    )


def adamw(parameter, first_state, second, clipped, rate):
    first_new = first_state + (1.0 - BETA_ONE) * clipped
    second_new = second + (1.0 - BETA_TWO) * clipped * clipped
    root = (1.0 - BETA_TWO**STEP) ** 0.5
    below = pl.reciprocal(second_new * lax.rsqrt(second_new) + ADAM_EPS * root)
    scale = rate * root / (1.0 - BETA_ONE**STEP)
    return parameter - scale * (first_new * below), first_new, second_new


def decay_kernel(w, m, v, pv, pm, pq, nw, nm, nv, npv, npm, npq):
    for ins, outs, rate in (
        ((w, m, v), (nw, nm, nv), LEARN_RATE),
        ((pv, pm, pq), (npv, npm, npq), VECTOR_RATE),
    ):
        for ref, out, scale in zip(ins, outs, (1.0 - rate * DECAY_RATE, BETA_ONE, BETA_TWO)):
            out[...] = ref[...] * scale


def decay(arrays, after):
    return call(
        decay_kernel,
        [(0, a) for a in arrays],
        [(a.shape, F32) for a in arrays],
        name="decay",
        vmem=4,
        after=after,
    )


def adamw_kernel(*refs):
    place = Place()
    sums, refs = refs[:2], refs[2:]
    (vgrad, w, m, v, pv, pm, pq), refs = refs[:7], refs[7:]
    wide, low, refs = refs[:4], refs[4:8], refs[8:]
    outs, (npv, npm, npq, norm), scrs, sems = refs[:4], refs[4:8], refs[8:12], refs[12]
    opt = place[0]
    total = sums[0][...] + sums[1][...]
    total = jnp.sum(jnp.sum(total, axis=1, keepdims=True), axis=0, keepdims=True)
    grad_norm = jnp.sqrt(total)
    factor = jnp.minimum(1.0, CLIP_NORM / (grad_norm + 1e-06))
    norm[...] = grad_norm
    for j in range(3):
        cols = slice(128 * j, 128 * j + 128)
        g = vgrad[16 * j : 16 * j + 16, :].astype(F32)
        g = jnp.where(opt == 0, g[0:6], g[6:12])
        a, b, c = adamw(pv[:, cols], pm[:, cols], pq[:, cols], g * factor, VECTOR_RATE)
        npv[:, cols] = a
        npm[:, cols] = b
        npq[:, cols] = c

    def block(grad, rows, cols):
        new = adamw(w[rows, cols], m[rows, cols], v[rows, cols], grad * factor, LEARN_RATE)
        for scr, value in zip(scrs, new + (new[0].astype(BF16),)):
            scr[rows, cols] = value

    def copies(r, i):
        rows = aligned(CHUNK * (place[1] ^ r) + i * 16, 16, 16)
        return [
            pltpu.make_async_copy(scr.at[rows, :], out.at[rows, :], sems.at[3 * r + i, j])
            for j, (scr, out) in enumerate(zip(scrs, outs))
        ]

    for r in range(4):

        def step(i, carry, r=r):
            rows = aligned(CHUNK * (place[1] ^ r) + i * 16, 16, 16)
            here = aligned(i * 16, 16, 16)
            for j in range(4):
                at = D * (place[3] ^ j)
                for p, start in enumerate((4 * D + FF, 4 * D)):
                    grad = wide[r][2 * j + p, here, :].astype(F32)
                    block(grad, rows, aligned(start + at, D, 128))
            for c in range(4):
                grad = low[r][here, D * c : D * c + D].astype(F32)
                block(grad, rows, slice(D * c, D * c + D))
            for copy in copies(r, i):
                copy.start()
            return carry

        lax.fori_loop(0, CHUNK // 16, step, 0)
    for r in range(4):

        def finish(i, carry, r=r):
            for copy in copies(r, i):
                copy.wait()
            return carry

        lax.fori_loop(0, CHUNK // 16, finish, 0)


def update(place, sums, vgrad, w, m, v, pv, pm, pq, parts):
    ins = tuple(sums) + (vgrad, w, m, v, pv, pm, pq) + tuple(parts)
    shapes = [(w.shape, F32)] * 3 + [(w.shape, BF16)] + [(pv.shape, F32)] * 3 + [((1, 1), F32)]
    return pl.pallas_call(
        adamw_kernel,
        out_shape=[jax.ShapeDtypeStruct(s, d) for s, d in shapes],
        in_specs=[VMEM] * len(ins),
        out_specs=[ANY] * 4 + [VMEM] * 4,
        scratch_shapes=[
            pltpu.VMEM(w.shape, F32),
            pltpu.VMEM(w.shape, F32),
            pltpu.VMEM(w.shape, F32),
            pltpu.VMEM(w.shape, BF16),
            pltpu.SemaphoreType.DMA((12, 4)),
        ],
        compiler_params=pltpu.CompilerParams(vmem_limit_bytes=16 << 20),
        cost_estimate=pl.CostEstimate(
            flops=4000000000, bytes_accessed=26 * w.size, transcendentals=0
        ),
        name="adamw",
    )(*ins)


def shards(
    n,
    tokens,
    lengths,
    query_index,
    doc_index,
    targets,
    weights,
    first_moment,
    second_moment,
    vectors,
    vec_first,
    vec_second,
):
    place = None
    scalars = jnp.concatenate([lengths.reshape(SEGS), query_index, doc_index, targets])
    groups = bit_groups(n)

    w_own, wo_own, wu_own, wd_own = cast(weights)
    w_other = pair(w_own)
    vectors_late, w_own = lax.optimization_barrier((vectors, w_own))
    v_other = pair(vectors_late)
    wo = (wo_own, pair(wo_own))
    wu = (wu_own, pair(wu_own))
    wd = (wd_own, pair(wd_own))

    proj, att, lse, segc, segr, ownc, ownr, wanted, marks, vec, wqkv = attend(
        place, scalars, (tokens, w_own, w_other, vectors, v_other)
    )
    xhat1, inv1, hlow, act, up_proj, xhat2, inv2, unit, uscale, wo, wu, wd = mlp(
        place, wanted, att, tokens, ownr, vec, wo + wu + wd
    )
    units, packed = pack(marks, unit, pair(unit))
    groups = bit_groups(n)
    order = [0]
    stack = packed
    for i, (shift, size) in enumerate(groups[1:] + groups[:1]):
        pieces = [stack] + [swap(stack, "dp", n, k << shift) for k in range(1, size)]
        order = [o | (k << shift) for k in range(size) for o in order]
        if i < len(groups) - 1:
            slope = slope_of(up_proj, [packed])
            stack = join(pieces, [slope]).reshape(-1, 2 * PAIRS, D + 128)
    decayed = decay(
        (weights, first_moment, second_moment, vectors, vec_first, vec_second), [packed]
    )
    dsec, dlow, keep, send, dsums = down_backward(
        n, order, place, wanted, units, ownc, uscale, (xhat2, inv2, act), vec, pieces,
        decayed,
    )
    other = pair(send)
    dup, ukeep, usend, usums = up_backward(place, dlow, slope, hlow, wd, [])
    down, go = pair_sum(1, keep, other, [dup])
    dother = swap(go, "dp", n, 1)
    up, go = pair_sum(2, ukeep, pair(usend), [down])
    uother = swap(go, "dp", n, 2)
    dfirst, datt, delta, okeep, osend, fsums = first_backward(
        place, dup, dsec, xhat1, inv1, att, vec, wu, wo, [up]
    )
    ins = (tokens, proj, datt, lse, delta, segc, segr)
    part0, keep0, send0, sums0 = heads_backward(0, place, ins, (), [])
    part1, keep1, send1, sums1 = heads_backward(1, place, ins, (), [part0])
    down, dsend, up, usend = wide_step((down, dother, up, uother), [part1])
    dother, uother = swap(dsend, "dp", n, 2), swap(usend, "dp", n, 1)
    part2, keep, send, _ = heads_backward(
        2, place, ins,
        (okeep, osend, keep0, send0, keep1, send1, dsums, usums, fsums, sums0, sums1),
        [down, part1],
    )
    other = pair(send)
    igrad = input_backward((part0, part1, part2), dfirst, wqkv, [part2])
    iother = pair(igrad)
    wide = wide_plane_sum(place, (down, dother, up, uother), [igrad])
    wide_got = trades(wide, n, 2)
    low = core_sum(keep, other, [wide[0]])
    low_got = trades(low, n, 0)
    wide = rest_sum(low_plane_sum(wide_got, [low[0]]), n)
    wide_got = trades([wide] * 4, n, 2)
    low = low_plane_sum(low_got, [wide])
    other = swap(low, "dp", n, 4)
    wide = chain(wide_got, [low])
    wide = trades([wide] * 4, n, 0)
    low = low_next(low, other, [wide[0]])
    other = swap(low, "dp", n, 8)
    input_grad, flag = merge(place, igrad, iother, [low])
    low, vgrad = low_last(low, other, [flag])
    low, vgrad = rest_sum(low, n), rest_sum(vgrad, n)
    low = trades([low] * 4, n, 0)
    sums = squares(place, low, vgrad, squares(place, wide, after=[low[0]]))
    sums = (sums, pair(sums))
    pieces = tuple(wide) + tuple(low)
    nw, nm, nv, nlow, npv, npm, npq, norm = update(
        place, sums, vgrad, *decayed, pieces,
    )
    return (norm.reshape(()), input_grad, nw, nm, nv, nlow, npv, npm, npq)


def solution(mesh):
    rows = P("opt", None)
    in_specs = (P("dp", None), P("dp", None), P("dp"), P("dp"), P("dp")) + (rows,) * 6
    out_specs = (P(), P("dp", None)) + (rows,) * 7
    n = mesh.shape["dp"]
    return jax.shard_map(
        functools.partial(shards, n),
        mesh=mesh,
        in_specs=in_specs,
        out_specs=out_specs,
        check_vma=False,
    )
```

profile of v0, /device:TPU:0, one launch (start us, length us, event | category | flops | bytes accessed | tf_op | source)
XLA Modules:
  0.0 109.0 jit_solution(12498292325986180037)
XLA Ops:
  0.7 2.2 %cast.1 = (bf16[192,1152]{1,0:T(8,128)(2,1)S(1)}, bf16[192,384]{1,0:T(8,128)(2,1)S(1)}, bf16[192,1536]{1,0:T(8,128)(2,1)S(1)}, bf16[192,1536]{1,0:T(8,128)(2,1)S(1)}) custom-call(f32[192,4608]{1,0:T(8,128)} %refs_0_.4), custom_call_target="tpu_custom_call" | custom-call | tf_op jit(solution)/shard_map/cast/pallas_call | solution.py:270
  4.8 5.8 %attend.1 = (bf16[640,1152]{1,0:T(8,128)(2,1)S(1)}, bf16[576,384]{1,0:T(8,128)(2,1)S(1)}, f32[3,4,640]{2,1,0:T(4,128)S(1)}, s32[576,128]{1,0:T(8,128)S(1)}, s32[...) custom-call(s32[40]{0:T(128)S(1)} %pad_add_fusion.refs_0_, ...), custom_call_target="tpu_custom_call" | custom-call | flops 8800000000 | bytes 5197984 | tf_op jit(solution)/shard_map/attend/pallas_call | solution.py:108
  10.6 5.2 %mlp.1 = (f32[576,384]{1,0:T(8,128)S(1)}, f32[576,128]{1,0:T(8,128)S(1)}, bf16[576,384]{1,0:T(8,128)(2,1)S(1)}, bf16[576,1536]{1,0:T(8,128)(2,1)S(1)}, f32[576,1...) custom-call(s32[2,16,128]{2,1,0:T(8,128)S(1)} %get-tuple-element.104, ...), custom_call_target="tpu_custom_call" | custom-call | flops 11000000512 | bytes 14741504 | tf_op jit(solution)/shard_map/mlp/pallas_call | solution.py:108
  16.2 0.8 collective-permute-done.5.refs_2_
  17.1 4.9 %collective-permute-start.8 = (bf16[16,512]{1,0:T(8,128)(2,1)S(1)}, bf16[16,512]{1,0:T(8,128)(2,1)S(1)}, u32[]{:S(2)}, u32[]{:S(2)}) collective-permute-start(bf16[16,512]{1,0:T(8,128)(2,1)S(1)} %get-tuple-element.119.refs_1_.refs_0_.refs_6_), channel_id=1, source_target_pairs={{0,24},{2,26},{4,28},{6,30},{8,16},{10,18},{12,20},{14,22},{16,8},... | collective-permute-start | bytes 49160 | tf_op jit(solution)/shard_map/ppermute | solution.py:721
  22.0 0.6 collective-permute-start.6
  22.7 1.5 %slope.1.refs_4_.refs_1_ = f32[576,1536]{1,0:T(8,128)S(1)} custom-call(f32[576,1536]{1,0:T(8,128)S(1)} %get-tuple-element.120.refs_0_, bf16[16,512]{1,0:T(8,128)(2,1)S(1)} %get-tuple-element.119.refs_1_.refs_0_.refs_6_), custom_call_target="tpu_custom_call" | custom-call | flops 5500000256 | bytes 7077888 | tf_op jit(solution)/shard_map/slope/pallas_call | solution.py:108
  24.2 2.4 %collective-permute-done.7.refs_2_ = bf16[16,512]{1,0:T(8,128)(2,1)S(1)} collective-permute-done((bf16[16,512]{1,0:T(8,128)(2,1)S(1)}, bf16[16,512]{1,0:T(8,128)(2,1)S(1)}, u32[]{:S(2)}, u32[]{:S(2)}) %collective-permute-start.7) | collective-permute-done | bytes 16416 | tf_op jit(solution)/shard_map/ppermute | solution.py:721
  26.7 2.5 %collective-permute-start.11 = (bf16[4,16,512]{2,1,0:T(8,128)(2,1)S(1)}, bf16[4,16,512]{2,1,0:T(8,128)(2,1)S(1)}, u32[]{:S(2)}, u32[]{:S(2)}) collective-permute-start(bf16[4,16,512]{2,1,0:T(8,128)(2,1)S(1)} %join.1.refs_8_), channel_id=1, source_target_pairs={{0,6},{2,4},{4,2},{6,0},{8,14},{10,12},{12,10},{14,8},{16,22},{18,... | collective-permute-start | bytes 196616 | tf_op jit(solution)/shard_map/ppermute | solution.py:721
  30.2 0.9 decay.1
  31.2 1.2 %collective-permute-done.11.refs_11_ = bf16[4,16,512]{2,1,0:T(8,128)(2,1)S(1)} collective-permute-done((bf16[4,16,512]{2,1,0:T(8,128)(2,1)S(1)}, bf16[4,16,512]{2,1,0:T(8,128)(2,1)S(1)}, u32[]{:S(2)}, u32[]{:S(2)}) %collective-permute-start.11) | collective-permute-done | bytes 65568 | tf_op jit(solution)/shard_map/ppermute | solution.py:721
  32.4 1.1 collective-permute-done.10.refs_10_
  34.0 3.7 %down_backward.1 = (f32[576,384]{1,0:T(8,128)S(1)}, bf16[576,384]{1,0:T(8,128)(2,1)S(1)}, bf16[4,4,48,384]{3,2,1,0:T(8,128)(2,1)S(1)}, bf16[4,4,48,384]{3,2,1,0:T(8,128)(2,1)S(1)}, f32[8,384]{1,0:T(8,128)S(1)}) custom-call(s32[2,16,128]{2,1,0:T(8,128)S(1)} %get-tuple-element.104.refs_0_, f32[16,384]{1,0:T(8,128)S(1)} %get-tuple-element.113.refs_1_, ...), custom_call_target="tpu_custom_call" | custom-call | flops 4400000000 | bytes 6098944 | tf_op jit(solution)/shard_map/down_backward/pallas_call | solution.py:108
  37.8 2.3 %up_backward.1 = (bf16[576,1536]{1,0:T(8,128)(2,1)S(1)}, bf16[4,4,48,384]{3,2,1,0:T(8,128)(2,1)S(1)}, bf16[4,4,48,384]{3,2,1,0:T(8,128)(2,1)S(1)}, f32[4,384]{1,0:T(4,128)S(1)}) custom-call(bf16[576,384]{1,0:T(8,128)(2,1)S(1)} %get-tuple-element.127.refs_0_, f32[576,1536]{1,0:T(8,128)S(1)} %slope.1.refs_4_.refs_1_, ...), custom_call_target="tpu_custom_call" | custom-call | flops 3300000000 | bytes 8558592 | tf_op jit(solution)/shard_map/up_backward/pallas_call | solution.py:108
  40.1 0.6 collective-permute-start.12
  40.8 1.5 %collective-permute-done.12.refs_1_ = bf16[4,4,48,384]{3,2,1,0:T(8,128)(2,1)S(1)} collective-permute-done((bf16[4,4,48,384]{3,2,1,0:T(8,128)(2,1)S(1)}, bf16[4,4,48,384]{3,2,1,0:T(8,128)(2,1)S(1)}, u32[]{:S(2)}, u32[]{:S(2)}) %collective-permute-start.12) | collective-permute-done | bytes 589856 | tf_op jit(solution)/shard_map/ppermute | solution.py:721
  42.4 1.6 %collective-permute-start.15 = (bf16[2,4,48,384]{3,2,1,0:T(8,128)(2,1)S(1)}, bf16[2,4,48,384]{3,2,1,0:T(8,128)(2,1)S(1)}, u32[]{:S(2)}, u32[]{:S(2)}) collective-permute-start(bf16[2,4,48,384]{3,2,1,0:T(8,128)(2,1)S(1)} %get-tuple-element.160), channel_id=1, source_target_pairs={{0,4},{2,6},{4,0},{6,2},{8,12},{10,14},{12,8},{14,10},{16,20},{18,... | collective-permute-start | bytes 884744 | tf_op jit(solution)/shard_map/ppermute | solution.py:721
  44.6 2.5 %first_backward.1 = (f32[576,384]{1,0:T(8,128)S(1)}, bf16[640,384]{1,0:T(8,128)(2,1)S(1)}, f32[16,640]{1,0:T(8,128)S(1)}, bf16[4,48,384]{2,1,0:T(8,128)(2,1)S(1)...) custom-call(bf16[576,1536]{1,0:T(8,128)(2,1)S(1)} %get-tuple-element.130.refs_2_.refs_0_, ...), custom_call_target="tpu_custom_call" | custom-call | flops 1100000000 | bytes 7499776 | tf_op jit(solution)/shard_map/first_backward/pallas_call | solution.py:108
  47.1 2.7 %heads_backward.3 = (bf16[576,384]{1,0:T(8,128)(2,1)S(1)}, bf16[4,48,384]{2,1,0:T(8,128)(2,1)S(1)}, bf16[4,48,384]{2,1,0:T(8,128)(2,1)S(1)}, f32[8,128]{1,0:T(8,128)S(1)}) custom-call(bf16[1024,384]{1,0:T(8,128)(2,1)S(1)} %copy-done.1, bf16[640,1152]{1,0:T(8,128)(2,1)S(1)} %get-tuple-element.103.refs_1_, bf16[640,384]{1,0:T(8,128)(2,1)S(1)} %get-tuple-element.142.refs_2_, ...), custom_call_target="tpu_custom_call" | custom-call | flops 1100000000 | bytes 3880960 | tf_op jit(solution)/shard_map/heads_backward/pallas_call | solution.py:108
  49.8 2.7 %heads_backward.4 = (bf16[576,384]{1,0:T(8,128)(2,1)S(1)}, bf16[4,48,384]{2,1,0:T(8,128)(2,1)S(1)}, bf16[4,48,384]{2,1,0:T(8,128)(2,1)S(1)}, f32[8,128]{1,0:T(8,128)S(1)}) custom-call(bf16[1024,384]{1,0:T(8,128)(2,1)S(1)} %copy-done.1, bf16[640,1152]{1,0:T(8,128)(2,1)S(1)} %get-tuple-element.103.refs_1_, bf16[640,384]{1,0:T(8,128)(2,1)S(1)} %get-tuple-element.142.refs_2_, ...), custom_call_target="tpu_custom_call" | custom-call | flops 1100000000 | bytes 3880960 | tf_op jit(solution)/shard_map/heads_backward/pallas_call | solution.py:108
  53.2 0.6 collective-permute-start.17
  53.8 1.0 collective-permute-start.18
  54.7 3.5 %heads_backward.5 = (bf16[576,384]{1,0:T(8,128)(2,1)S(1)}, bf16[4,48,1664]{2,1,0:T(8,128)(2,1)S(1)}, bf16[4,48,1664]{2,1,0:T(8,128)(2,1)S(1)}, f32[8,128]{1,0:T(8,128)}) custom-call(bf16[1024,384]{1,0:T(8,128)(2,1)S(1)} %copy-done.1, bf16[640,1152]{1,0:T(8,128)(2,1)S(1)} %get-tuple-element.103.refs_1_, bf16[640,384]{1,0:T(8,128)(2,1)S(1)} %get-tuple-element.142.refs_2_, ...), custom_call_target="tpu_custom_call" | custom-call | flops 1100000000 | bytes 5787648 | tf_op jit(solution)/shard_map/heads_backward/pallas_call | solution.py:108
  58.3 0.9 input_backward.1.refs_4_.refs_0_
  59.2 0.6 collective-permute-start.30
  59.9 2.0 %collective-permute-start.23 = (bf16[2,48,384]{2,1,0:T(8,128)(2,1)S(1)}, bf16[2,48,384]{2,1,0:T(8,128)(2,1)S(1)}, u32[]{:S(2)}, u32[]{:S(2)}) collective-permute-start(bf16[2,48,384]{2,1,0:T(8,128)(2,1)S(1)} %get-tuple-element.177), channel_id=1, source_target_pairs={{0,16},{2,18},{4,20},{6,22},{8,24},{10,26},{12,28},{14,30},{16,0},... | collective-permute-start | bytes 221192 | tf_op jit(solution)/shard_map/ppermute | solution.py:721
  61.9 2.3 %collective-permute-start.24 = (bf16[2,48,384]{2,1,0:T(8,128)(2,1)S(1)}, bf16[2,48,384]{2,1,0:T(8,128)(2,1)S(1)}, u32[]{:S(2)}, u32[]{:S(2)}) collective-permute-start(bf16[2,48,384]{2,1,0:T(8,128)(2,1)S(1)} %get-tuple-element.178), channel_id=1, source_target_pairs={{0,24},{2,26},{4,28},{6,30},{8,16},{10,18},{12,20},{14,22},{16,8},... | collective-permute-start | bytes 221192 | tf_op jit(solution)/shard_map/ppermute | solution.py:721
  64.4 1.1 %collective-permute-start.19 = (bf16[48,1664]{1,0:T(8,128)(2,1)S(1)}, bf16[48,1664]{1,0:T(8,128)(2,1)S(1)}, u32[]{:S(2)}, u32[]{:S(2)}) collective-permute-start(bf16[48,1664]{1,0:T(8,128)(2,1)S(1)} %get-tuple-element.173), channel_id=1, source_target_pairs={{0,2},{2,0},{4,6},{6,4},{8,10},{10,8},{12,14},{14,12},{16,18},{18,... | collective-permute-start | bytes 479240 | tf_op jit(solution)/shard_map/ppermute | solution.py:721
  65.7 1.5 %collective-permute-start.20 = (bf16[48,1664]{1,0:T(8,128)(2,1)S(1)}, bf16[48,1664]{1,0:T(8,128)(2,1)S(1)}, u32[]{:S(2)}, u32[]{:S(2)}) collective-permute-start(bf16[48,1664]{1,0:T(8,128)(2,1)S(1)} %get-tuple-element.174), channel_id=1, source_target_pairs={{0,4},{2,6},{4,0},{6,2},{8,12},{10,14},{12,8},{14,10},{16,20},{18,... | collective-permute-start | bytes 479240 | tf_op jit(solution)/shard_map/ppermute | solution.py:721
  67.2 1.2 %collective-permute-start.21 = (bf16[48,1664]{1,0:T(8,128)(2,1)S(1)}, bf16[48,1664]{1,0:T(8,128)(2,1)S(1)}, u32[]{:S(2)}, u32[]{:S(2)}) collective-permute-start(bf16[48,1664]{1,0:T(8,128)(2,1)S(1)} %get-tuple-element.175), channel_id=1, source_target_pairs={{0,6},{2,4},{4,2},{6,0},{8,14},{10,12},{12,10},{14,8},{16,22},{18,... | collective-permute-start | bytes 479240 | tf_op jit(solution)/shard_map/ppermute | solution.py:721
  68.8 4.6 %collective-permute-start.28 = (bf16[2,48,384]{2,1,0:T(8,128)(2,1)S(1)}, bf16[2,48,384]{2,1,0:T(8,128)(2,1)S(1)}, u32[]{:S(2)}, u32[]{:S(2)}) collective-permute-start(bf16[2,48,384]{2,1,0:T(8,128)(2,1)S(1)} %low_plane_sum.2.refs_4_.refs_0_), channel_id=1, source_target_pairs={{0,24},{2,26},{4,28},{6,30},{8,16},{10,18},{12,20},{14,22},{16,8},... | collective-permute-start | bytes 221192 | tf_op jit(solution)/shard_map/ppermute | solution.py:721
  73.4 1.0 collective-permute-done.20.refs_2_
  74.5 2.1 %collective-permute-start.25 = (bf16[48,1664]{1,0:T(8,128)(2,1)S(1)}, bf16[48,1664]{1,0:T(8,128)(2,1)S(1)}, u32[]{:S(2)}, u32[]{:S(2)}) collective-permute-start(bf16[48,1664]{1,0:T(8,128)(2,1)S(1)} %low_plane_sum.3.refs_4_.refs_0_), channel_id=1, source_target_pairs={{0,8},{2,10},{4,12},{6,14},{8,0},{10,2},{12,4},{14,6},{16,24},{18,... | collective-permute-start | bytes 479240 | tf_op jit(solution)/shard_map/ppermute | solution.py:721
  76.5 2.7 %collective-permute-done.27.refs_2_ = bf16[2,48,384]{2,1,0:T(8,128)(2,1)S(1)} collective-permute-done((bf16[2,48,384]{2,1,0:T(8,128)(2,1)S(1)}, bf16[2,48,384]{2,1,0:T(8,128)(2,1)S(1)}, u32[]{:S(2)}, u32[]{:S(2)}) %collective-permute-start.27) | collective-permute-done | bytes 73760 | tf_op jit(solution)/shard_map/ppermute | solution.py:721
  79.3 1.5 %collective-permute-done.26.refs_1_ = bf16[2,48,384]{2,1,0:T(8,128)(2,1)S(1)} collective-permute-done((bf16[2,48,384]{2,1,0:T(8,128)(2,1)S(1)}, bf16[2,48,384]{2,1,0:T(8,128)(2,1)S(1)}, u32[]{:S(2)}, u32[]{:S(2)}) %collective-permute-start.26) | collective-permute-done | bytes 73760 | tf_op jit(solution)/shard_map/ppermute | solution.py:721
  80.8 1.3 %collective-permute-start.36 = (bf16[8,48,384]{2,1,0:T(8,128)(2,1)S(1)}, bf16[8,48,384]{2,1,0:T(8,128)(2,1)S(1)}, u32[]{:S(2)}, u32[]{:S(2)}) collective-permute-start(bf16[8,48,384]{2,1,0:T(8,128)(2,1)S(1)} %chain.1.refs_2_.refs_0_.refs_9_), channel_id=1, source_target_pairs={{0,6},{2,4},{4,2},{6,0},{8,14},{10,12},{12,10},{14,8},{16,22},{18,... | collective-permute-start | bytes 884744 | tf_op jit(solution)/shard_map/ppermute | solution.py:721
  82.1 1.1 %collective-permute-start.35 = (bf16[8,48,384]{2,1,0:T(8,128)(2,1)S(1)}, bf16[8,48,384]{2,1,0:T(8,128)(2,1)S(1)}, u32[]{:S(2)}, u32[]{:S(2)}) collective-permute-start(bf16[8,48,384]{2,1,0:T(8,128)(2,1)S(1)} %chain.1.refs_2_.refs_0_.refs_9_), channel_id=1, source_target_pairs={{0,4},{2,6},{4,0},{6,2},{8,12},{10,14},{12,8},{14,10},{16,20},{18,... | collective-permute-start | bytes 884744 | tf_op jit(solution)/shard_map/ppermute | solution.py:721
  83.2 1.1 %collective-permute-start.34 = (bf16[8,48,384]{2,1,0:T(8,128)(2,1)S(1)}, bf16[8,48,384]{2,1,0:T(8,128)(2,1)S(1)}, u32[]{:S(2)}, u32[]{:S(2)}) collective-permute-start(bf16[8,48,384]{2,1,0:T(8,128)(2,1)S(1)} %chain.1.refs_2_.refs_0_.refs_9_), channel_id=1, source_target_pairs={{0,2},{2,0},{4,6},{6,4},{8,10},{10,8},{12,14},{14,12},{16,18},{18,... | collective-permute-start | bytes 884744 | tf_op jit(solution)/shard_map/ppermute | solution.py:721
  84.9 1.0 merge.1
  85.9 6.5 %collective-permute-done.29.refs_1_ = bf16[48,1664]{1,0:T(8,128)(2,1)S(1)} collective-permute-done((bf16[48,1664]{1,0:T(8,128)(2,1)S(1)}, bf16[48,1664]{1,0:T(8,128)(2,1)S(1)}, u32[]{:S(2)}, u32[]{:S(2)}) %collective-permute-start.29) | collective-permute-done | bytes 159776 | tf_op jit(solution)/shard_map/ppermute | solution.py:721
  92.4 1.3 %collective-permute-start.33 = (bf16[48,1536]{1,0:T(8,128)(2,1)S(1)}, bf16[48,1536]{1,0:T(8,128)(2,1)S(1)}, u32[]{:S(2)}, u32[]{:S(2)}) collective-permute-start(bf16[48,1536]{1,0:T(8,128)(2,1)S(1)} %get-tuple-element.180.refs_4_.refs_0_.refs_13_), channel_id=1, source_target_pairs={{0,6},{2,4},{4,2},{6,0},{8,14},{10,12},{12,10},{14,8},{16,22},{18,... | collective-permute-start | bytes 442376 | tf_op jit(solution)/shard_map/ppermute | solution.py:721
  93.7 1.2 %collective-permute-start.32 = (bf16[48,1536]{1,0:T(8,128)(2,1)S(1)}, bf16[48,1536]{1,0:T(8,128)(2,1)S(1)}, u32[]{:S(2)}, u32[]{:S(2)}) collective-permute-start(bf16[48,1536]{1,0:T(8,128)(2,1)S(1)} %get-tuple-element.180.refs_4_.refs_0_.refs_13_), channel_id=1, source_target_pairs={{0,4},{2,6},{4,0},{6,2},{8,12},{10,14},{12,8},{14,10},{16,20},{18,... | collective-permute-start | bytes 442376 | tf_op jit(solution)/shard_map/ppermute | solution.py:721
  94.9 1.0 collective-permute-start.31
  95.9 1.1 collective-permute-done.35.refs_2_.refs_11_
  97.4 2.8 %collective-permute-done.33.refs_3_.refs_16_ = bf16[48,1536]{1,0:T(8,128)(2,1)S(1)} collective-permute-done((bf16[48,1536]{1,0:T(8,128)(2,1)S(1)}, bf16[48,1536]{1,0:T(8,128)(2,1)S(1)}, u32[]{:S(2)}, u32[]{:S(2)}) %collective-permute-start.33) | collective-permute-done | bytes 147488 | tf_op jit(solution)/shard_map/ppermute | solution.py:721
  100.2 1.4 %collective-permute-done.32.refs_2_.refs_15_ = bf16[48,1536]{1,0:T(8,128)(2,1)S(1)} collective-permute-done((bf16[48,1536]{1,0:T(8,128)(2,1)S(1)}, bf16[48,1536]{1,0:T(8,128)(2,1)S(1)}, u32[]{:S(2)}, u32[]{:S(2)}) %collective-permute-start.32) | collective-permute-done | bytes 147488 | tf_op jit(solution)/shard_map/ppermute | solution.py:721
  101.9 1.2 %collective-permute-done.37.refs_1_ = f32[8,128]{1,0:T(8,128)S(1)} collective-permute-done((f32[8,128]{1,0:T(8,128)S(1)}, f32[8,128]{1,0:T(8,128)S(1)}, u32[]{:S(2)}, u32[]{:S(2)}) %collective-permute-start.37) | collective-permute-done | bytes 4128 | tf_op jit(solution)/shard_map/ppermute | solution.py:721
  103.0 5.8 %adamw.1 = (f32[192,4608]{1,0:T(8,128)}, f32[192,4608]{1,0:T(8,128)}, f32[192,4608]{1,0:T(8,128)}, bf16[192,4608]{1,0:T(8,128)(2,1)}, f32[6,384]{1,0:T(8,128)}, ...) custom-call(f32[8,128]{1,0:T(8,128)S(1)} %squares.3.refs_0_, f32[8,128]{1,0:T(8,128)S(1)} %collective-permute-done.37.refs_1_, ...), custom_call_target="tpu_custom_call" | custom-call | flops 4000000000 | bytes 23003136 | tf_op jit(solution)/shard_map/adamw/pallas_call | solution.py:1078
  (79 shorter events, 7.8 us)
Async XLA Ops:
  0.7 3.8 %copy-start.7 = (s32[8]{0:T(128)S(1)}, s32[8]{0:T(128)}, u32[]{:S(2)}) copy-start(s32[8]{0:T(128)} %param.15) | copy-start | bytes 100
  0.7 3.8 %copy-start.8 = (s32[8]{0:T(128)S(1)}, s32[8]{0:T(128)}, u32[]{:S(2)}) copy-start(s32[8]{0:T(128)} %param.14) | copy-start | bytes 100
  0.7 3.7 %copy-start.9 = (s32[8]{0:T(128)S(1)}, s32[8]{0:T(128)}, u32[]{:S(2)}) copy-start(s32[8]{0:T(128)} %param.13) | copy-start | bytes 100
  0.7 3.7 %copy-start.10 = (s32[1,16]{1,0:T(1,128)S(1)}, s32[1,16]{1,0:T(1,128)}, u32[]{:S(2)}) copy-start(s32[1,16]{1,0:T(1,128)} %param.12) | copy-start | bytes 196
  0.7 4.1 %copy-start.1 = (bf16[1024,384]{1,0:T(8,128)(2,1)S(1)}, bf16[1024,384]{1,0:T(8,128)(2,1)}, u32[]{:S(2)}) copy-start(bf16[1024,384]{1,0:T(8,128)(2,1)} %refs_0_.7) | copy-start | bytes 2359300
  2.9 2.0 %collective-permute-start = (bf16[192,1152]{1,0:T(8,128)(2,1)S(1)}, bf16[192,1152]{1,0:T(8,128)(2,1)S(1)}, u32[]{:S(2)}, u32[]{:S(2)}) collective-permute-start(bf16[192,1152]{1,0:T(8,128)(2,1)S(1)} %get-tuple-element.101.refs_2_), channel_id=1, source_target_pairs={{0,1},{1,0},{2,3},{3,2},{4,5},{5,4},{6,7},{7,6},{8,9},{9,8},{10,11... | collective-permute-start | bytes 1327112 | tf_op jit(solution)/shard_map/ppermute | solution.py:721
  3.4 1.4 %collective-permute-start.1 = (f32[6,384]{1,0:T(8,128)S(1)}, f32[6,384]{1,0:T(8,128)S(1)}, u32[]{:S(2)}, u32[]{:S(2)}) collective-permute-start(f32[6,384]{1,0:T(8,128)S(1)} %copy-done.4), channel_id=1, source_target_pairs={{0,1},{1,0},{2,3},{3,2},{4,5},{5,4},{6,7},{7,6},{8,9},{9,8},{10,11... | collective-permute-start | bytes 27656 | tf_op jit(solution)/shard_map/ppermute | solution.py:721
  3.5 7.1 %collective-permute-start.2 = (bf16[192,384]{1,0:T(8,128)(2,1)S(1)}, bf16[192,384]{1,0:T(8,128)(2,1)S(1)}, u32[]{:S(2)}, u32[]{:S(2)}) collective-permute-start(bf16[192,384]{1,0:T(8,128)(2,1)S(1)} %get-tuple-element.109.refs_5_), channel_id=1, source_target_pairs={{0,1},{1,0},{2,3},{3,2},{4,5},{5,4},{6,7},{7,6},{8,9},{9,8},{10,11... | collective-permute-start | bytes 442376 | tf_op jit(solution)/shard_map/ppermute | solution.py:721
  3.9 6.7 %collective-permute-start.3 = (bf16[192,1536]{1,0:T(8,128)(2,1)S(1)}, bf16[192,1536]{1,0:T(8,128)(2,1)S(1)}, u32[]{:S(2)}, u32[]{:S(2)}) collective-permute-start(bf16[192,1536]{1,0:T(8,128)(2,1)S(1)} %get-tuple-element.110.refs_7_), channel_id=1, source_target_pairs={{0,1},{1,0},{2,3},{3,2},{4,5},{5,4},{6,7},{7,6},{8,9},{9,8},{10,11... | collective-permute-start | bytes 1769480 | tf_op jit(solution)/shard_map/ppermute | solution.py:721
  4.0 6.6 %collective-permute-start.4 = (bf16[192,1536]{1,0:T(8,128)(2,1)S(1)}, bf16[192,1536]{1,0:T(8,128)(2,1)S(1)}, u32[]{:S(2)}, u32[]{:S(2)}) collective-permute-start(bf16[192,1536]{1,0:T(8,128)(2,1)S(1)} %get-tuple-element.111.refs_9_), channel_id=1, source_target_pairs={{0,1},{1,0},{2,3},{3,2},{4,5},{5,4},{6,7},{7,6},{8,9},{9,8},{10,11... | collective-permute-start | bytes 1769480 | tf_op jit(solution)/shard_map/ppermute | solution.py:721
  15.8 1.2 %collective-permute-start.5 = (f32[16,384]{1,0:T(8,128)S(1)}, f32[16,384]{1,0:T(8,128)S(1)}, u32[]{:S(2)}, u32[]{:S(2)}) collective-permute-start(f32[16,384]{1,0:T(8,128)S(1)} %get-tuple-element.112.refs_1_), channel_id=1, source_target_pairs={{0,1},{1,0},{2,3},{3,2},{4,5},{5,4},{6,7},{7,6},{8,9},{9,8},{10,11... | collective-permute-start | bytes 73736 | tf_op jit(solution)/shard_map/ppermute | solution.py:721
  17.1 7.2 %collective-permute-start.8 = (bf16[16,512]{1,0:T(8,128)(2,1)S(1)}, bf16[16,512]{1,0:T(8,128)(2,1)S(1)}, u32[]{:S(2)}, u32[]{:S(2)}) collective-permute-start(bf16[16,512]{1,0:T(8,128)(2,1)S(1)} %get-tuple-element.119.refs_1_.refs_0_.refs_6_), channel_id=1, source_target_pairs={{0,24},{2,26},{4,28},{6,30},{8,16},{10,18},{12,20},{14,22},{16,8},... | collective-permute-start | bytes 49160 | tf_op jit(solution)/shard_map/ppermute | solution.py:721
  22.0 4.6 %collective-permute-start.7 = (bf16[16,512]{1,0:T(8,128)(2,1)S(1)}, bf16[16,512]{1,0:T(8,128)(2,1)S(1)}, u32[]{:S(2)}, u32[]{:S(2)}) collective-permute-start(bf16[16,512]{1,0:T(8,128)(2,1)S(1)} %get-tuple-element.119.refs_1_.refs_0_.refs_6_), channel_id=1, source_target_pairs={{0,16},{2,18},{4,20},{6,22},{8,24},{10,26},{12,28},{14,30},{16,0},... | collective-permute-start | bytes 49160 | tf_op jit(solution)/shard_map/ppermute | solution.py:721
  22.0 4.6 %collective-permute-start.6 = (bf16[16,512]{1,0:T(8,128)(2,1)S(1)}, bf16[16,512]{1,0:T(8,128)(2,1)S(1)}, u32[]{:S(2)}, u32[]{:S(2)}) collective-permute-start(bf16[16,512]{1,0:T(8,128)(2,1)S(1)} %get-tuple-element.119.refs_1_.refs_0_.refs_6_), channel_id=1, source_target_pairs={{0,8},{2,10},{4,12},{6,14},{8,0},{10,2},{12,4},{14,6},{16,24},{18,... | collective-permute-start | bytes 49160 | tf_op jit(solution)/shard_map/ppermute | solution.py:721
  24.2 6.1 %copy-start = (f32[192,4608]{1,0:T(8,128)S(1)}, f32[192,4608]{1,0:T(8,128)}, u32[]{:S(2)}) copy-start(f32[192,4608]{1,0:T(8,128)} %refs_0_.4) | copy-start | bytes 10616836
  24.2 6.0 %copy-start.2 = (f32[192,4608]{1,0:T(8,128)S(1)}, f32[192,4608]{1,0:T(8,128)}, u32[]{:S(2)}) copy-start(f32[192,4608]{1,0:T(8,128)} %refs_1_.3) | copy-start | bytes 10616836
  24.2 6.0 %copy-start.3 = (f32[192,4608]{1,0:T(8,128)S(1)}, f32[192,4608]{1,0:T(8,128)}, u32[]{:S(2)}) copy-start(f32[192,4608]{1,0:T(8,128)} %refs_2_.3) | copy-start | bytes 10616836
  24.2 6.0 %copy-start.5 = (f32[6,384]{1,0:T(8,128)S(1)}, f32[6,384]{1,0:T(8,128)}, u32[]{:S(2)}) copy-start(f32[6,384]{1,0:T(8,128)} %refs_4_.3) | copy-start | bytes 27652
  24.2 6.0 %copy-start.6 = (f32[6,384]{1,0:T(8,128)S(1)}, f32[6,384]{1,0:T(8,128)}, u32[]{:S(2)}) copy-start(f32[6,384]{1,0:T(8,128)} %refs_5_.1) | copy-start | bytes 27652
  26.7 5.7 %collective-permute-start.11 = (bf16[4,16,512]{2,1,0:T(8,128)(2,1)S(1)}, bf16[4,16,512]{2,1,0:T(8,128)(2,1)S(1)}, u32[]{:S(2)}, u32[]{:S(2)}) collective-permute-start(bf16[4,16,512]{2,1,0:T(8,128)(2,1)S(1)} %join.1.refs_8_), channel_id=1, source_target_pairs={{0,6},{2,4},{4,2},{6,0},{8,14},{10,12},{12,10},{14,8},{16,22},{18,... | collective-permute-start | bytes 196616 | tf_op jit(solution)/shard_map/ppermute | solution.py:721
  29.2 4.3 %collective-permute-start.10 = (bf16[4,16,512]{2,1,0:T(8,128)(2,1)S(1)}, bf16[4,16,512]{2,1,0:T(8,128)(2,1)S(1)}, u32[]{:S(2)}, u32[]{:S(2)}) collective-permute-start(bf16[4,16,512]{2,1,0:T(8,128)(2,1)S(1)} %join.1.refs_8_), channel_id=1, source_target_pairs={{0,4},{2,6},{4,0},{6,2},{8,12},{10,14},{12,8},{14,10},{16,20},{18,... | collective-permute-start | bytes 196616 | tf_op jit(solution)/shard_map/ppermute | solution.py:721
  29.7 4.3 %collective-permute-start.9 = (bf16[4,16,512]{2,1,0:T(8,128)(2,1)S(1)}, bf16[4,16,512]{2,1,0:T(8,128)(2,1)S(1)}, u32[]{:S(2)}, u32[]{:S(2)}) collective-permute-start(bf16[4,16,512]{2,1,0:T(8,128)(2,1)S(1)} %join.1.refs_8_), channel_id=1, source_target_pairs={{0,2},{2,0},{4,6},{6,4},{8,10},{10,8},{12,14},{14,12},{16,18},{18,... | collective-permute-start | bytes 196616 | tf_op jit(solution)/shard_map/ppermute | solution.py:721
  37.7 3.0 %collective-permute-start.13 = (bf16[4,4,48,384]{3,2,1,0:T(8,128)(2,1)S(1)}, bf16[4,4,48,384]{3,2,1,0:T(8,128)(2,1)S(1)}, u32[]{:S(2)}, u32[]{:S(2)}) collective-permute-start(bf16[4,4,48,384]{3,2,1,0:T(8,128)(2,1)S(1)} %get-tuple-element.139), channel_id=1, source_target_pairs={{0,1},{1,0},{2,3},{3,2},{4,5},{5,4},{6,7},{7,6},{8,9},{9,8},{10,11... | collective-permute-start | bytes 1769480 | tf_op jit(solution)/shard_map/ppermute | solution.py:721
  40.1 2.2 %collective-permute-start.12 = (bf16[4,4,48,384]{3,2,1,0:T(8,128)(2,1)S(1)}, bf16[4,4,48,384]{3,2,1,0:T(8,128)(2,1)S(1)}, u32[]{:S(2)}, u32[]{:S(2)}) collective-permute-start(bf16[4,4,48,384]{3,2,1,0:T(8,128)(2,1)S(1)} %get-tuple-element.137), channel_id=1, source_target_pairs={{0,1},{1,0},{2,3},{3,2},{4,5},{5,4},{6,7},{7,6},{8,9},{9,8},{10,11... | collective-permute-start | bytes 1769480 | tf_op jit(solution)/shard_map/ppermute | solution.py:721
  42.4 10.0 %collective-permute-start.15 = (bf16[2,4,48,384]{3,2,1,0:T(8,128)(2,1)S(1)}, bf16[2,4,48,384]{3,2,1,0:T(8,128)(2,1)S(1)}, u32[]{:S(2)}, u32[]{:S(2)}) collective-permute-start(bf16[2,4,48,384]{3,2,1,0:T(8,128)(2,1)S(1)} %get-tuple-element.160), channel_id=1, source_target_pairs={{0,4},{2,6},{4,0},{6,2},{8,12},{10,14},{12,8},{14,10},{16,20},{18,... | collective-permute-start | bytes 884744 | tf_op jit(solution)/shard_map/ppermute | solution.py:721
  44.0 9.0 %collective-permute-start.14 = (bf16[2,4,48,384]{3,2,1,0:T(8,128)(2,1)S(1)}, bf16[2,4,48,384]{3,2,1,0:T(8,128)(2,1)S(1)}, u32[]{:S(2)}, u32[]{:S(2)}) collective-permute-start(bf16[2,4,48,384]{3,2,1,0:T(8,128)(2,1)S(1)} %get-tuple-element.159), channel_id=1, source_target_pairs={{0,2},{2,0},{4,6},{6,4},{8,10},{10,8},{12,14},{14,12},{16,18},{18,... | collective-permute-start | bytes 884744 | tf_op jit(solution)/shard_map/ppermute | solution.py:721
  53.2 6.6 %collective-permute-start.17 = (bf16[4,48,384]{2,1,0:T(8,128)(2,1)S(1)}, bf16[4,48,384]{2,1,0:T(8,128)(2,1)S(1)}, u32[]{:S(2)}, u32[]{:S(2)}) collective-permute-start(bf16[4,48,384]{2,1,0:T(8,128)(2,1)S(1)} %get-tuple-element.165), channel_id=1, source_target_pairs={{0,4},{2,6},{4,0},{6,2},{8,12},{10,14},{12,8},{14,10},{16,20},{18,... | collective-permute-start | bytes 442376 | tf_op jit(solution)/shard_map/ppermute | solution.py:721
  53.8 6.0 %collective-permute-start.18 = (bf16[4,48,384]{2,1,0:T(8,128)(2,1)S(1)}, bf16[4,48,384]{2,1,0:T(8,128)(2,1)S(1)}, u32[]{:S(2)}, u32[]{:S(2)}) collective-permute-start(bf16[4,48,384]{2,1,0:T(8,128)(2,1)S(1)} %get-tuple-element.167), channel_id=1, source_target_pairs={{0,2},{2,0},{4,6},{6,4},{8,10},{10,8},{12,14},{14,12},{16,18},{18,... | collective-permute-start | bytes 442376 | tf_op jit(solution)/shard_map/ppermute | solution.py:721
  58.2 6.0 %collective-permute-start.16 = (bf16[4,48,1664]{2,1,0:T(8,128)(2,1)S(1)}, bf16[4,48,1664]{2,1,0:T(8,128)(2,1)S(1)}, u32[]{:S(2)}, u32[]{:S(2)}) collective-permute-start(bf16[4,48,1664]{2,1,0:T(8,128)(2,1)S(1)} %get-tuple-element.164), channel_id=1, source_target_pairs={{0,1},{1,0},{2,3},{3,2},{4,5},{5,4},{6,7},{7,6},{8,9},{9,8},{10,11... | collective-permute-start | bytes 1916936 | tf_op jit(solution)/shard_map/ppermute | solution.py:721
  59.2 25.7 %collective-permute-start.30 = (bf16[576,384]{1,0:T(8,128)(2,1)S(1)}, bf16[576,384]{1,0:T(8,128)(2,1)S(1)}, u32[]{:S(2)}, u32[]{:S(2)}) collective-permute-start(bf16[576,384]{1,0:T(8,128)(2,1)S(1)} %input_backward.1.refs_4_.refs_0_), channel_id=1, source_target_pairs={{0,1},{1,0},{2,3},{3,2},{4,5},{5,4},{6,7},{7,6},{8,9},{9,8},{10,11... | collective-permute-start | bytes 1327112 | tf_op jit(solution)/shard_map/ppermute | solution.py:721
  59.8 5.8 %collective-permute-start.22 = (bf16[2,48,384]{2,1,0:T(8,128)(2,1)S(1)}, bf16[2,48,384]{2,1,0:T(8,128)(2,1)S(1)}, u32[]{:S(2)}, u32[]{:S(2)}) collective-permute-start(bf16[2,48,384]{2,1,0:T(8,128)(2,1)S(1)} %get-tuple-element.176), channel_id=1, source_target_pairs={{0,8},{2,10},{4,12},{6,14},{8,0},{10,2},{12,4},{14,6},{16,24},{18,... | collective-permute-start | bytes 221192 | tf_op jit(solution)/shard_map/ppermute | solution.py:721
  59.9 7.3 %collective-permute-start.23 = (bf16[2,48,384]{2,1,0:T(8,128)(2,1)S(1)}, bf16[2,48,384]{2,1,0:T(8,128)(2,1)S(1)}, u32[]{:S(2)}, u32[]{:S(2)}) collective-permute-start(bf16[2,48,384]{2,1,0:T(8,128)(2,1)S(1)} %get-tuple-element.177), channel_id=1, source_target_pairs={{0,16},{2,18},{4,20},{6,22},{8,24},{10,26},{12,28},{14,30},{16,0},... | collective-permute-start | bytes 221192 | tf_op jit(solution)/shard_map/ppermute | solution.py:721
  61.9 6.8 %collective-permute-start.24 = (bf16[2,48,384]{2,1,0:T(8,128)(2,1)S(1)}, bf16[2,48,384]{2,1,0:T(8,128)(2,1)S(1)}, u32[]{:S(2)}, u32[]{:S(2)}) collective-permute-start(bf16[2,48,384]{2,1,0:T(8,128)(2,1)S(1)} %get-tuple-element.178), channel_id=1, source_target_pairs={{0,24},{2,26},{4,28},{6,30},{8,16},{10,18},{12,20},{14,22},{16,8},... | collective-permute-start | bytes 221192 | tf_op jit(solution)/shard_map/ppermute | solution.py:721
  64.4 8.9 %collective-permute-start.19 = (bf16[48,1664]{1,0:T(8,128)(2,1)S(1)}, bf16[48,1664]{1,0:T(8,128)(2,1)S(1)}, u32[]{:S(2)}, u32[]{:S(2)}) collective-permute-start(bf16[48,1664]{1,0:T(8,128)(2,1)S(1)} %get-tuple-element.173), channel_id=1, source_target_pairs={{0,2},{2,0},{4,6},{6,4},{8,10},{10,8},{12,14},{14,12},{16,18},{18,... | collective-permute-start | bytes 479240 | tf_op jit(solution)/shard_map/ppermute | solution.py:721
  65.7 8.7 %collective-permute-start.20 = (bf16[48,1664]{1,0:T(8,128)(2,1)S(1)}, bf16[48,1664]{1,0:T(8,128)(2,1)S(1)}, u32[]{:S(2)}, u32[]{:S(2)}) collective-permute-start(bf16[48,1664]{1,0:T(8,128)(2,1)S(1)} %get-tuple-element.174), channel_id=1, source_target_pairs={{0,4},{2,6},{4,0},{6,2},{8,12},{10,14},{12,8},{14,10},{16,20},{18,... | collective-permute-start | bytes 479240 | tf_op jit(solution)/shard_map/ppermute | solution.py:721
  67.2 7.2 %collective-permute-start.21 = (bf16[48,1664]{1,0:T(8,128)(2,1)S(1)}, bf16[48,1664]{1,0:T(8,128)(2,1)S(1)}, u32[]{:S(2)}, u32[]{:S(2)}) collective-permute-start(bf16[48,1664]{1,0:T(8,128)(2,1)S(1)} %get-tuple-element.175), channel_id=1, source_target_pairs={{0,6},{2,4},{4,2},{6,0},{8,14},{10,12},{12,10},{14,8},{16,22},{18,... | collective-permute-start | bytes 479240 | tf_op jit(solution)/shard_map/ppermute | solution.py:721
  68.8 7.8 %collective-permute-start.28 = (bf16[2,48,384]{2,1,0:T(8,128)(2,1)S(1)}, bf16[2,48,384]{2,1,0:T(8,128)(2,1)S(1)}, u32[]{:S(2)}, u32[]{:S(2)}) collective-permute-start(bf16[2,48,384]{2,1,0:T(8,128)(2,1)S(1)} %low_plane_sum.2.refs_4_.refs_0_), channel_id=1, source_target_pairs={{0,24},{2,26},{4,28},{6,30},{8,16},{10,18},{12,20},{14,22},{16,8},... | collective-permute-start | bytes 221192 | tf_op jit(solution)/shard_map/ppermute | solution.py:721
  73.4 5.9 %collective-permute-start.27 = (bf16[2,48,384]{2,1,0:T(8,128)(2,1)S(1)}, bf16[2,48,384]{2,1,0:T(8,128)(2,1)S(1)}, u32[]{:S(2)}, u32[]{:S(2)}) collective-permute-start(bf16[2,48,384]{2,1,0:T(8,128)(2,1)S(1)} %low_plane_sum.2.refs_4_.refs_0_), channel_id=1, source_target_pairs={{0,16},{2,18},{4,20},{6,22},{8,24},{10,26},{12,28},{14,30},{16,0},... | collective-permute-start | bytes 221192 | tf_op jit(solution)/shard_map/ppermute | solution.py:721
  74.4 6.4 %collective-permute-start.26 = (bf16[2,48,384]{2,1,0:T(8,128)(2,1)S(1)}, bf16[2,48,384]{2,1,0:T(8,128)(2,1)S(1)}, u32[]{:S(2)}, u32[]{:S(2)}) collective-permute-start(bf16[2,48,384]{2,1,0:T(8,128)(2,1)S(1)} %low_plane_sum.2.refs_4_.refs_0_), channel_id=1, source_target_pairs={{0,8},{2,10},{4,12},{6,14},{8,0},{10,2},{12,4},{14,6},{16,24},{18,... | collective-permute-start | bytes 221192 | tf_op jit(solution)/shard_map/ppermute | solution.py:721
  74.5 9.9 %collective-permute-start.25 = (bf16[48,1664]{1,0:T(8,128)(2,1)S(1)}, bf16[48,1664]{1,0:T(8,128)(2,1)S(1)}, u32[]{:S(2)}, u32[]{:S(2)}) collective-permute-start(bf16[48,1664]{1,0:T(8,128)(2,1)S(1)} %low_plane_sum.3.refs_4_.refs_0_), channel_id=1, source_target_pairs={{0,8},{2,10},{4,12},{6,14},{8,0},{10,2},{12,4},{14,6},{16,24},{18,... | collective-permute-start | bytes 479240 | tf_op jit(solution)/shard_map/ppermute | solution.py:721
  80.8 14.1 %collective-permute-start.36 = (bf16[8,48,384]{2,1,0:T(8,128)(2,1)S(1)}, bf16[8,48,384]{2,1,0:T(8,128)(2,1)S(1)}, u32[]{:S(2)}, u32[]{:S(2)}) collective-permute-start(bf16[8,48,384]{2,1,0:T(8,128)(2,1)S(1)} %chain.1.refs_2_.refs_0_.refs_9_), channel_id=1, source_target_pairs={{0,6},{2,4},{4,2},{6,0},{8,14},{10,12},{12,10},{14,8},{16,22},{18,... | collective-permute-start | bytes 884744 | tf_op jit(solution)/shard_map/ppermute | solution.py:721
  82.1 14.9 %collective-permute-start.35 = (bf16[8,48,384]{2,1,0:T(8,128)(2,1)S(1)}, bf16[8,48,384]{2,1,0:T(8,128)(2,1)S(1)}, u32[]{:S(2)}, u32[]{:S(2)}) collective-permute-start(bf16[8,48,384]{2,1,0:T(8,128)(2,1)S(1)} %chain.1.refs_2_.refs_0_.refs_9_), channel_id=1, source_target_pairs={{0,4},{2,6},{4,0},{6,2},{8,12},{10,14},{12,8},{14,10},{16,20},{18,... | collective-permute-start | bytes 884744 | tf_op jit(solution)/shard_map/ppermute | solution.py:721
  83.2 14.1 %collective-permute-start.34 = (bf16[8,48,384]{2,1,0:T(8,128)(2,1)S(1)}, bf16[8,48,384]{2,1,0:T(8,128)(2,1)S(1)}, u32[]{:S(2)}, u32[]{:S(2)}) collective-permute-start(bf16[8,48,384]{2,1,0:T(8,128)(2,1)S(1)} %chain.1.refs_2_.refs_0_.refs_9_), channel_id=1, source_target_pairs={{0,2},{2,0},{4,6},{6,4},{8,10},{10,8},{12,14},{14,12},{16,18},{18,... | collective-permute-start | bytes 884744 | tf_op jit(solution)/shard_map/ppermute | solution.py:721
  84.4 8.0 %collective-permute-start.29 = (bf16[48,1664]{1,0:T(8,128)(2,1)S(1)}, bf16[48,1664]{1,0:T(8,128)(2,1)S(1)}, u32[]{:S(2)}, u32[]{:S(2)}) collective-permute-start(bf16[48,1664]{1,0:T(8,128)(2,1)S(1)} %low_next.1.refs_2_.refs_0_), channel_id=1, source_target_pairs={{0,16},{2,18},{4,20},{6,22},{8,24},{10,26},{12,28},{14,30},{16,0},... | collective-permute-start | bytes 479240 | tf_op jit(solution)/shard_map/ppermute | solution.py:721
  92.4 7.8 %collective-permute-start.33 = (bf16[48,1536]{1,0:T(8,128)(2,1)S(1)}, bf16[48,1536]{1,0:T(8,128)(2,1)S(1)}, u32[]{:S(2)}, u32[]{:S(2)}) collective-permute-start(bf16[48,1536]{1,0:T(8,128)(2,1)S(1)} %get-tuple-element.180.refs_4_.refs_0_.refs_13_), channel_id=1, source_target_pairs={{0,6},{2,4},{4,2},{6,0},{8,14},{10,12},{12,10},{14,8},{16,22},{18,... | collective-permute-start | bytes 442376 | tf_op jit(solution)/shard_map/ppermute | solution.py:721
  93.7 8.0 %collective-permute-start.32 = (bf16[48,1536]{1,0:T(8,128)(2,1)S(1)}, bf16[48,1536]{1,0:T(8,128)(2,1)S(1)}, u32[]{:S(2)}, u32[]{:S(2)}) collective-permute-start(bf16[48,1536]{1,0:T(8,128)(2,1)S(1)} %get-tuple-element.180.refs_4_.refs_0_.refs_13_), channel_id=1, source_target_pairs={{0,4},{2,6},{4,0},{6,2},{8,12},{10,14},{12,8},{14,10},{16,20},{18,... | collective-permute-start | bytes 442376 | tf_op jit(solution)/shard_map/ppermute | solution.py:721
  94.9 6.8 %collective-permute-start.31 = (bf16[48,1536]{1,0:T(8,128)(2,1)S(1)}, bf16[48,1536]{1,0:T(8,128)(2,1)S(1)}, u32[]{:S(2)}, u32[]{:S(2)}) collective-permute-start(bf16[48,1536]{1,0:T(8,128)(2,1)S(1)} %get-tuple-element.180.refs_4_.refs_0_.refs_13_), channel_id=1, source_target_pairs={{0,2},{2,0},{4,6},{6,4},{8,10},{10,8},{12,14},{14,12},{16,18},{18,... | collective-permute-start | bytes 442376 | tf_op jit(solution)/shard_map/ppermute | solution.py:721
  101.8 1.2 %collective-permute-start.37 = (f32[8,128]{1,0:T(8,128)S(1)}, f32[8,128]{1,0:T(8,128)S(1)}, u32[]{:S(2)}, u32[]{:S(2)}) collective-permute-start(f32[8,128]{1,0:T(8,128)S(1)} %squares.3.refs_0_), channel_id=1, source_target_pairs={{0,1},{1,0},{2,3},{3,2},{4,5},{5,4},{6,7},{7,6},{8,9},{9,8},{10,11... | collective-permute-start | bytes 12296 | tf_op jit(solution)/shard_map/ppermute | solution.py:721
  (1 other events, 2.7 us)
where the time goes:
time: 109 us
  Pallas kernels  41.8 us (38%)
  starting transfers between devices  38.6 us (35%)
  waiting for transfers between devices  27.3 us (25%)
  between operations  1.14 us (1%)
    ppermute x38, starting transfers between devices, swap(): return lax.ppermute(value, axis, flips(axis, size, bits))  38.6 us
    pallas_call x26, Pallas kernels, call(): pl.pallas_call(body, out_shape=shapes, in_specs=specs, out_specs=[VMEM] *...  33.9 us
    ppermute x38, waiting for transfers between devices, swap(): return lax.ppermute(value, axis, flips(axis, size, bits))  27.3 us
    pallas_call x1, Pallas kernels, update(): pl.pallas_call(adamw_kernel, out_shape=[jax.ShapeDtypeStruct(s, d) for s,...  5.82 us
  transfers between devices with their start and end apart: 38, of which 20 were waited for; matrix products, arithmetic and copies ran while one was open for 0% of the time, Pallas kernels for 23%

commit v1 on v0

--- a/solution.py
+++ b/solution.py
@@ -180,9 +180,9 @@
         proj[0:WIN, cols] = (nn(x, wfull[:, cols]) + bias_row[:, cols]).astype(BF16)
     proj[WIN:PAD, :] = jnp.zeros((PAD - WIN, 3 * D), BF16)
 
-    def group(g, carry):
+    def group(g):
         def lanes(part):
-            return aligned(part * D + 128 * g, 128, 128)
+            return slice(part * D + 128 * g, part * D + 128 * g + 128)
 
         for t in range(PAD // 128):
             vt[:, 128 * t : 128 * t + 128] = (
@@ -214,12 +214,12 @@
                     outs.append(o[0:HD, 0:BLOCK] * totals[-2])
                     outs.append(o[HD : 2 * HD, BLOCK : 2 * BLOCK] * totals[-1])
             rows = min(BLOCK, WIN - q0)
-            att[q0 : q0 + rows, aligned(128 * g, 128, 128)] = (
+            att[q0 : q0 + rows, lanes(0)] = (
                 jnp.concatenate(outs, axis=0).T[0:rows].astype(BF16)
             )
-        return carry
-
-    lax.fori_loop(0, 3, group, 0)
+
+    for g in range(3):
+        group(g)
 
 
 def attend(place, scalars, arrays):
@@ -304,10 +304,13 @@
         inverse = lax.rsqrt(jnp.mean(centred * centred, axis=1, keepdims=True) + LN_EPS)
         return centred * inverse, inverse
 
-    def block(i, carry):
-        r = aligned(i * WIDE_ROWS, WIDE_ROWS, 64)
+    branch = nn(att[0:WIDE_ROWS, :], wo[...])
+    for i in range(WIN // WIDE_ROWS):
+        r = slice(i * WIDE_ROWS, (i + 1) * WIDE_ROWS)
         x = tokens[aligned(OFF * opt + i * WIDE_ROWS, WIDE_ROWS, 64), :].astype(F32)
-        normed, inverse = norm(nn(att[r, :], wo[...]) + vec[2:3, :] + x)
+        normed, inverse = norm(branch + vec[2:3, :] + x)
+        if i + 1 < WIN // WIDE_ROWS:
+            branch = nn(att[(i + 1) * WIDE_ROWS : (i + 2) * WIDE_ROWS, :], wo[...])
         xhat1[r, :] = normed
         inv1[r, :] = jnp.broadcast_to(inverse, (WIDE_ROWS, 128))
         h = normed * vec[8:9, :] + vec[9:10, :]
@@ -328,9 +331,6 @@
         high, rest = low_pair(normed * vec[10:11, :] + vec[11:12, :])
         ench[r, :] = high
         encl[r, :] = rest
-        return carry
-
-    lax.fori_loop(0, WIN // WIDE_ROWS, block, 0)
 
     onehot = jnp.where(wanted[0, :, 0:1] == ownr[0:1, 0:WIN], 1.0, 0.0)
     count = jnp.maximum(jnp.sum(onehot, axis=1, keepdims=True), 1.0)
@@ -458,11 +458,13 @@
     hot = jnp.where(ownc[:, 0 : 2 * PAIRS] == wanted[1, 0:1, 0 : 2 * PAIRS], 1.0, 0.0).astype(BF16)
     high, rest_low = low_pair(d_pool)
     dsec[...] = nn(hot, high) + nn(hot, rest_low)
-    norm_backward(lambda r: dsec[r, :], xhat2, inv2, vec[10:11, :], dsec, dlow, sums, 0)
+    norm_backward(
+        lambda r: dsec[r, :], xhat2, inv2, vec[10:11, :], dsec, dlow, sums, 0, WIDE_ROWS
+    )
     sums[3:8, :] = jnp.zeros((5, D), F32)
-    for c in range(3):
-        cols = slice(c * 512, (c + 1) * 512)
-        grad[:, cols] = tn(dlow[...], act[:, cols])
+    halves = [slice(0, 2 * D), slice(2 * D, 4 * D)]
+    grad[:, halves[0]] = tn(dlow[...], act[:, halves[0]])
+    grad[:, halves[1]] = tn(dlow[...], act[:, halves[1]])
     for c in range(4):
         split_rows(grad.at[:, c * D : (c + 1) * D], keep, send, place, c)
 
@@ -495,17 +497,16 @@
 
 
 def up_kernel(place, dlow, slope, hlow, wd, dup, keep, send, sums, grad):
-    coming = nn(dlow[...], wd[:, 0:512])
-    for c in range(3):
-        cols = slice(c * 512, (c + 1) * 512)
+    coming = nn(dlow[...], wd[:, 0 : 2 * D])
+    for c in range(2):
+        cols = slice(c * 2 * D, (c + 1) * 2 * D)
         part = (coming * slope[:, cols]).astype(BF16)
-        if c < 2:
-            coming = nn(dlow[...], wd[:, (c + 1) * 512 : (c + 2) * 512])
+        if c == 0:
+            coming = nn(dlow[...], wd[:, 2 * D : 4 * D])
         dup[:, cols] = part
         column_sum = jnp.sum(part.astype(F32), axis=0, keepdims=True)
-        for j in range(4):
-            at = 512 * c + 128 * j
-            sums[at // D : at // D + 1, at % D : at % D + 128] = column_sum[:, 128 * j : 128 * j + 128]
+        for j in range(2):
+            sums[2 * c + j : 2 * c + j + 1, :] = column_sum[:, j * D : (j + 1) * D]
         grad[:, cols] = tn(hlow[...], dup[:, cols])
     for c in range(4):
         split_rows(grad.at[:, c * D : (c + 1) * D], keep, send, place, c)

time: 109 us -> 107 us (0.982)
  Pallas kernels: 41.8 us -> 39.8 us
    pallas_call x26, Pallas kernels: 33.9 us -> 31.8 us  [call(): pl.pallas_call(body, out_shape=shapes, in_specs=specs, out_specs=[VMEM] *...]
  transfers between devices with their start and end apart: 38 -> 38, of which waited for: 20 -> 20; matrix products, arithmetic and copies ran while one was open for 0% -> 0% of each run, Pallas kernels for 23% -> 22%
where the time goes in v1:
time: 107 us
  Pallas kernels  39.8 us (37%)
  starting transfers between devices  38.5 us (36%)
  waiting for transfers between devices  27.4 us (26%)
  between operations  1.14 us (1%)
    ppermute x38, starting transfers between devices, swap(): return lax.ppermute(value, axis, flips(axis, size, bits))  38.5 us
    pallas_call x26, Pallas kernels, call(): pl.pallas_call(body, out_shape=shapes, in_specs=specs, out_specs=[VMEM] *...  31.8 us
    ppermute x38, waiting for transfers between devices, swap(): return lax.ppermute(value, axis, flips(axis, size, bits))  27.4 us
    pallas_call x1, Pallas kernels, update(): pl.pallas_call(adamw_kernel, out_shape=[jax.ShapeDtypeStruct(s, d) for s,...  5.82 us
    pallas_call x1, Pallas kernels, cast(): pl.pallas_call(cast_kernel, out_shape=[jax.ShapeDtypeStruct((HALF, c), BF...  2.15 us
  transfers between devices with their start and end apart: 38, of which 20 were waited for; matrix products, arithmetic and copies ran while one was open for 0% of the time, Pallas kernels for 22%

profile of v1, /device:TPU:0, one launch (start us, length us, event | category | flops | bytes accessed | tf_op | source)
XLA Modules:
  0.0 107.0 jit_solution(12769511277783020293)
XLA Ops:
  0.7 2.2 %cast.1 = (bf16[192,1152]{1,0:T(8,128)(2,1)S(1)}, bf16[192,384]{1,0:T(8,128)(2,1)S(1)}, bf16[192,1536]{1,0:T(8,128)(2,1)S(1)}, bf16[192,1536]{1,0:T(8,128)(2,1)S(1)}) custom-call(f32[192,4608]{1,0:T(8,128)} %refs_0_.4), custom_call_target="tpu_custom_call" | custom-call | tf_op jit(solution)/shard_map/cast/pallas_call | solution.py:270
  4.8 5.1 %attend.1 = (bf16[640,1152]{1,0:T(8,128)(2,1)S(1)}, bf16[576,384]{1,0:T(8,128)(2,1)S(1)}, f32[3,4,640]{2,1,0:T(4,128)S(1)}, s32[576,128]{1,0:T(8,128)S(1)}, s32[...) custom-call(s32[40]{0:T(128)S(1)} %pad_add_fusion.refs_0_, ...), custom_call_target="tpu_custom_call" | custom-call | flops 8800000000 | bytes 5197984 | tf_op jit(solution)/shard_map/attend/pallas_call | solution.py:108
  9.9 4.3 %mlp.1 = (f32[576,384]{1,0:T(8,128)S(1)}, f32[576,128]{1,0:T(8,128)S(1)}, bf16[576,384]{1,0:T(8,128)(2,1)S(1)}, bf16[576,1536]{1,0:T(8,128)(2,1)S(1)}, f32[576,1...) custom-call(s32[2,16,128]{2,1,0:T(8,128)S(1)} %get-tuple-element.104, ...), custom_call_target="tpu_custom_call" | custom-call | flops 11000000512 | bytes 14741504 | tf_op jit(solution)/shard_map/mlp/pallas_call | solution.py:108
  14.7 0.8 collective-permute-done.5.refs_2_
  15.6 4.9 %collective-permute-start.8 = (bf16[16,512]{1,0:T(8,128)(2,1)S(1)}, bf16[16,512]{1,0:T(8,128)(2,1)S(1)}, u32[]{:S(2)}, u32[]{:S(2)}) collective-permute-start(bf16[16,512]{1,0:T(8,128)(2,1)S(1)} %get-tuple-element.119.refs_1_.refs_0_.refs_6_), channel_id=1, source_target_pairs={{0,24},{2,26},{4,28},{6,30},{8,16},{10,18},{12,20},{14,22},{16,8},... | collective-permute-start | bytes 49160 | tf_op jit(solution)/shard_map/ppermute | solution.py:722
  20.5 0.6 collective-permute-start.6
  21.1 1.5 %slope.1.refs_4_.refs_1_ = f32[576,1536]{1,0:T(8,128)S(1)} custom-call(f32[576,1536]{1,0:T(8,128)S(1)} %get-tuple-element.120.refs_0_, bf16[16,512]{1,0:T(8,128)(2,1)S(1)} %get-tuple-element.119.refs_1_.refs_0_.refs_6_), custom_call_target="tpu_custom_call" | custom-call | flops 5500000256 | bytes 7077888 | tf_op jit(solution)/shard_map/slope/pallas_call | solution.py:108
  22.7 2.4 %collective-permute-done.7.refs_2_ = bf16[16,512]{1,0:T(8,128)(2,1)S(1)} collective-permute-done((bf16[16,512]{1,0:T(8,128)(2,1)S(1)}, bf16[16,512]{1,0:T(8,128)(2,1)S(1)}, u32[]{:S(2)}, u32[]{:S(2)}) %collective-permute-start.7) | collective-permute-done | bytes 16416 | tf_op jit(solution)/shard_map/ppermute | solution.py:722
  25.1 2.5 %collective-permute-start.11 = (bf16[4,16,512]{2,1,0:T(8,128)(2,1)S(1)}, bf16[4,16,512]{2,1,0:T(8,128)(2,1)S(1)}, u32[]{:S(2)}, u32[]{:S(2)}) collective-permute-start(bf16[4,16,512]{2,1,0:T(8,128)(2,1)S(1)} %join.1.refs_8_), channel_id=1, source_target_pairs={{0,6},{2,4},{4,2},{6,0},{8,14},{10,12},{12,10},{14,8},{16,22},{18,... | collective-permute-start | bytes 196616 | tf_op jit(solution)/shard_map/ppermute | solution.py:722
  28.7 0.9 decay.1
  29.6 1.1 %collective-permute-done.11.refs_11_ = bf16[4,16,512]{2,1,0:T(8,128)(2,1)S(1)} collective-permute-done((bf16[4,16,512]{2,1,0:T(8,128)(2,1)S(1)}, bf16[4,16,512]{2,1,0:T(8,128)(2,1)S(1)}, u32[]{:S(2)}, u32[]{:S(2)}) %collective-permute-start.11) | collective-permute-done | bytes 65568 | tf_op jit(solution)/shard_map/ppermute | solution.py:722
  30.8 1.1 %collective-permute-done.10.refs_10_ = bf16[4,16,512]{2,1,0:T(8,128)(2,1)S(1)} collective-permute-done((bf16[4,16,512]{2,1,0:T(8,128)(2,1)S(1)}, bf16[4,16,512]{2,1,0:T(8,128)(2,1)S(1)}, u32[]{:S(2)}, u32[]{:S(2)}) %collective-permute-start.10) | collective-permute-done | bytes 65568 | tf_op jit(solution)/shard_map/ppermute | solution.py:722
  32.4 3.2 %down_backward.1 = (f32[576,384]{1,0:T(8,128)S(1)}, bf16[576,384]{1,0:T(8,128)(2,1)S(1)}, bf16[4,4,48,384]{3,2,1,0:T(8,128)(2,1)S(1)}, bf16[4,4,48,384]{3,2,1,0:T(8,128)(2,1)S(1)}, f32[8,384]{1,0:T(8,128)S(1)}) custom-call(s32[2,16,128]{2,1,0:T(8,128)S(1)} %get-tuple-element.104.refs_0_, f32[16,384]{1,0:T(8,128)S(1)} %get-tuple-element.113.refs_1_, ...), custom_call_target="tpu_custom_call" | custom-call | flops 4400000000 | bytes 6098944 | tf_op jit(solution)/shard_map/down_backward/pallas_call | solution.py:108
  35.7 2.3 %up_backward.1 = (bf16[576,1536]{1,0:T(8,128)(2,1)S(1)}, bf16[4,4,48,384]{3,2,1,0:T(8,128)(2,1)S(1)}, bf16[4,4,48,384]{3,2,1,0:T(8,128)(2,1)S(1)}, f32[4,384]{1,0:T(4,128)S(1)}) custom-call(bf16[576,384]{1,0:T(8,128)(2,1)S(1)} %get-tuple-element.127.refs_0_, f32[576,1536]{1,0:T(8,128)S(1)} %slope.1.refs_4_.refs_1_, ...), custom_call_target="tpu_custom_call" | custom-call | flops 3300000000 | bytes 8558592 | tf_op jit(solution)/shard_map/up_backward/pallas_call | solution.py:108
  38.1 0.6 collective-permute-start.12
  38.8 1.5 %collective-permute-done.12.refs_1_ = bf16[4,4,48,384]{3,2,1,0:T(8,128)(2,1)S(1)} collective-permute-done((bf16[4,4,48,384]{3,2,1,0:T(8,128)(2,1)S(1)}, bf16[4,4,48,384]{3,2,1,0:T(8,128)(2,1)S(1)}, u32[]{:S(2)}, u32[]{:S(2)}) %collective-permute-start.12) | collective-permute-done | bytes 589856 | tf_op jit(solution)/shard_map/ppermute | solution.py:722
  40.4 1.6 %collective-permute-start.15 = (bf16[2,4,48,384]{3,2,1,0:T(8,128)(2,1)S(1)}, bf16[2,4,48,384]{3,2,1,0:T(8,128)(2,1)S(1)}, u32[]{:S(2)}, u32[]{:S(2)}) collective-permute-start(bf16[2,4,48,384]{3,2,1,0:T(8,128)(2,1)S(1)} %get-tuple-element.160), channel_id=1, source_target_pairs={{0,4},{2,6},{4,0},{6,2},{8,12},{10,14},{12,8},{14,10},{16,20},{18,... | collective-permute-start | bytes 884744 | tf_op jit(solution)/shard_map/ppermute | solution.py:722
  42.5 2.5 %first_backward.1 = (f32[576,384]{1,0:T(8,128)S(1)}, bf16[640,384]{1,0:T(8,128)(2,1)S(1)}, f32[16,640]{1,0:T(8,128)S(1)}, bf16[4,48,384]{2,1,0:T(8,128)(2,1)S(1)...) custom-call(bf16[576,1536]{1,0:T(8,128)(2,1)S(1)} %get-tuple-element.130.refs_2_.refs_0_, ...), custom_call_target="tpu_custom_call" | custom-call | flops 1100000000 | bytes 7499776 | tf_op jit(solution)/shard_map/first_backward/pallas_call | solution.py:108
  45.0 2.7 %heads_backward.3 = (bf16[576,384]{1,0:T(8,128)(2,1)S(1)}, bf16[4,48,384]{2,1,0:T(8,128)(2,1)S(1)}, bf16[4,48,384]{2,1,0:T(8,128)(2,1)S(1)}, f32[8,128]{1,0:T(8,128)S(1)}) custom-call(bf16[1024,384]{1,0:T(8,128)(2,1)S(1)} %copy-done.1, bf16[640,1152]{1,0:T(8,128)(2,1)S(1)} %get-tuple-element.103.refs_1_, bf16[640,384]{1,0:T(8,128)(2,1)S(1)} %get-tuple-element.142.refs_2_, ...), custom_call_target="tpu_custom_call" | custom-call | flops 1100000000 | bytes 3880960 | tf_op jit(solution)/shard_map/heads_backward/pallas_call | solution.py:108
  47.8 2.7 %heads_backward.4 = (bf16[576,384]{1,0:T(8,128)(2,1)S(1)}, bf16[4,48,384]{2,1,0:T(8,128)(2,1)S(1)}, bf16[4,48,384]{2,1,0:T(8,128)(2,1)S(1)}, f32[8,128]{1,0:T(8,128)S(1)}) custom-call(bf16[1024,384]{1,0:T(8,128)(2,1)S(1)} %copy-done.1, bf16[640,1152]{1,0:T(8,128)(2,1)S(1)} %get-tuple-element.103.refs_1_, bf16[640,384]{1,0:T(8,128)(2,1)S(1)} %get-tuple-element.142.refs_2_, ...), custom_call_target="tpu_custom_call" | custom-call | flops 1100000000 | bytes 3880960 | tf_op jit(solution)/shard_map/heads_backward/pallas_call | solution.py:108
  51.2 0.6 collective-permute-start.17
  51.7 1.0 collective-permute-start.18
  52.7 3.5 %heads_backward.5 = (bf16[576,384]{1,0:T(8,128)(2,1)S(1)}, bf16[4,48,1664]{2,1,0:T(8,128)(2,1)S(1)}, bf16[4,48,1664]{2,1,0:T(8,128)(2,1)S(1)}, f32[8,128]{1,0:T(8,128)}) custom-call(bf16[1024,384]{1,0:T(8,128)(2,1)S(1)} %copy-done.1, bf16[640,1152]{1,0:T(8,128)(2,1)S(1)} %get-tuple-element.103.refs_1_, bf16[640,384]{1,0:T(8,128)(2,1)S(1)} %get-tuple-element.142.refs_2_, ...), custom_call_target="tpu_custom_call" | custom-call | flops 1100000000 | bytes 5787648 | tf_op jit(solution)/shard_map/heads_backward/pallas_call | solution.py:108
  56.2 0.9 input_backward.1.refs_4_.refs_0_
  57.1 0.6 collective-permute-start.30
  57.9 2.0 %collective-permute-start.23 = (bf16[2,48,384]{2,1,0:T(8,128)(2,1)S(1)}, bf16[2,48,384]{2,1,0:T(8,128)(2,1)S(1)}, u32[]{:S(2)}, u32[]{:S(2)}) collective-permute-start(bf16[2,48,384]{2,1,0:T(8,128)(2,1)S(1)} %get-tuple-element.177), channel_id=1, source_target_pairs={{0,16},{2,18},{4,20},{6,22},{8,24},{10,26},{12,28},{14,30},{16,0},... | collective-permute-start | bytes 221192 | tf_op jit(solution)/shard_map/ppermute | solution.py:722
  59.9 2.3 %collective-permute-start.24 = (bf16[2,48,384]{2,1,0:T(8,128)(2,1)S(1)}, bf16[2,48,384]{2,1,0:T(8,128)(2,1)S(1)}, u32[]{:S(2)}, u32[]{:S(2)}) collective-permute-start(bf16[2,48,384]{2,1,0:T(8,128)(2,1)S(1)} %get-tuple-element.178), channel_id=1, source_target_pairs={{0,24},{2,26},{4,28},{6,30},{8,16},{10,18},{12,20},{14,22},{16,8},... | collective-permute-start | bytes 221192 | tf_op jit(solution)/shard_map/ppermute | solution.py:722
  62.4 1.1 %collective-permute-start.19 = (bf16[48,1664]{1,0:T(8,128)(2,1)S(1)}, bf16[48,1664]{1,0:T(8,128)(2,1)S(1)}, u32[]{:S(2)}, u32[]{:S(2)}) collective-permute-start(bf16[48,1664]{1,0:T(8,128)(2,1)S(1)} %get-tuple-element.173), channel_id=1, source_target_pairs={{0,2},{2,0},{4,6},{6,4},{8,10},{10,8},{12,14},{14,12},{16,18},{18,... | collective-permute-start | bytes 479240 | tf_op jit(solution)/shard_map/ppermute | solution.py:722
  63.7 1.5 %collective-permute-start.20 = (bf16[48,1664]{1,0:T(8,128)(2,1)S(1)}, bf16[48,1664]{1,0:T(8,128)(2,1)S(1)}, u32[]{:S(2)}, u32[]{:S(2)}) collective-permute-start(bf16[48,1664]{1,0:T(8,128)(2,1)S(1)} %get-tuple-element.174), channel_id=1, source_target_pairs={{0,4},{2,6},{4,0},{6,2},{8,12},{10,14},{12,8},{14,10},{16,20},{18,... | collective-permute-start | bytes 479240 | tf_op jit(solution)/shard_map/ppermute | solution.py:722
  65.2 1.1 %collective-permute-start.21 = (bf16[48,1664]{1,0:T(8,128)(2,1)S(1)}, bf16[48,1664]{1,0:T(8,128)(2,1)S(1)}, u32[]{:S(2)}, u32[]{:S(2)}) collective-permute-start(bf16[48,1664]{1,0:T(8,128)(2,1)S(1)} %get-tuple-element.175), channel_id=1, source_target_pairs={{0,6},{2,4},{4,2},{6,0},{8,14},{10,12},{12,10},{14,8},{16,22},{18,... | collective-permute-start | bytes 479240 | tf_op jit(solution)/shard_map/ppermute | solution.py:722
  66.8 4.6 %collective-permute-start.28 = (bf16[2,48,384]{2,1,0:T(8,128)(2,1)S(1)}, bf16[2,48,384]{2,1,0:T(8,128)(2,1)S(1)}, u32[]{:S(2)}, u32[]{:S(2)}) collective-permute-start(bf16[2,48,384]{2,1,0:T(8,128)(2,1)S(1)} %low_plane_sum.2.refs_4_.refs_0_), channel_id=1, source_target_pairs={{0,24},{2,26},{4,28},{6,30},{8,16},{10,18},{12,20},{14,22},{16,8},... | collective-permute-start | bytes 221192 | tf_op jit(solution)/shard_map/ppermute | solution.py:722
  71.4 1.0 collective-permute-done.20.refs_2_
  72.4 2.1 %collective-permute-start.25 = (bf16[48,1664]{1,0:T(8,128)(2,1)S(1)}, bf16[48,1664]{1,0:T(8,128)(2,1)S(1)}, u32[]{:S(2)}, u32[]{:S(2)}) collective-permute-start(bf16[48,1664]{1,0:T(8,128)(2,1)S(1)} %low_plane_sum.3.refs_4_.refs_0_), channel_id=1, source_target_pairs={{0,8},{2,10},{4,12},{6,14},{8,0},{10,2},{12,4},{14,6},{16,24},{18,... | collective-permute-start | bytes 479240 | tf_op jit(solution)/shard_map/ppermute | solution.py:722
  74.5 2.7 %collective-permute-done.27.refs_2_ = bf16[2,48,384]{2,1,0:T(8,128)(2,1)S(1)} collective-permute-done((bf16[2,48,384]{2,1,0:T(8,128)(2,1)S(1)}, bf16[2,48,384]{2,1,0:T(8,128)(2,1)S(1)}, u32[]{:S(2)}, u32[]{:S(2)}) %collective-permute-start.27) | collective-permute-done | bytes 73760 | tf_op jit(solution)/shard_map/ppermute | solution.py:722
  77.3 1.5 %collective-permute-done.26.refs_1_ = bf16[2,48,384]{2,1,0:T(8,128)(2,1)S(1)} collective-permute-done((bf16[2,48,384]{2,1,0:T(8,128)(2,1)S(1)}, bf16[2,48,384]{2,1,0:T(8,128)(2,1)S(1)}, u32[]{:S(2)}, u32[]{:S(2)}) %collective-permute-start.26) | collective-permute-done | bytes 73760 | tf_op jit(solution)/shard_map/ppermute | solution.py:722
  78.8 1.3 %collective-permute-start.36 = (bf16[8,48,384]{2,1,0:T(8,128)(2,1)S(1)}, bf16[8,48,384]{2,1,0:T(8,128)(2,1)S(1)}, u32[]{:S(2)}, u32[]{:S(2)}) collective-permute-start(bf16[8,48,384]{2,1,0:T(8,128)(2,1)S(1)} %chain.1.refs_2_.refs_0_.refs_9_), channel_id=1, source_target_pairs={{0,6},{2,4},{4,2},{6,0},{8,14},{10,12},{12,10},{14,8},{16,22},{18,... | collective-permute-start | bytes 884744 | tf_op jit(solution)/shard_map/ppermute | solution.py:722
  80.0 1.2 %collective-permute-start.35 = (bf16[8,48,384]{2,1,0:T(8,128)(2,1)S(1)}, bf16[8,48,384]{2,1,0:T(8,128)(2,1)S(1)}, u32[]{:S(2)}, u32[]{:S(2)}) collective-permute-start(bf16[8,48,384]{2,1,0:T(8,128)(2,1)S(1)} %chain.1.refs_2_.refs_0_.refs_9_), channel_id=1, source_target_pairs={{0,4},{2,6},{4,0},{6,2},{8,12},{10,14},{12,8},{14,10},{16,20},{18,... | collective-permute-start | bytes 884744 | tf_op jit(solution)/shard_map/ppermute | solution.py:722
  81.2 1.1 %collective-permute-start.34 = (bf16[8,48,384]{2,1,0:T(8,128)(2,1)S(1)}, bf16[8,48,384]{2,1,0:T(8,128)(2,1)S(1)}, u32[]{:S(2)}, u32[]{:S(2)}) collective-permute-start(bf16[8,48,384]{2,1,0:T(8,128)(2,1)S(1)} %chain.1.refs_2_.refs_0_.refs_9_), channel_id=1, source_target_pairs={{0,2},{2,0},{4,6},{6,4},{8,10},{10,8},{12,14},{14,12},{16,18},{18,... | collective-permute-start | bytes 884744 | tf_op jit(solution)/shard_map/ppermute | solution.py:722
  82.9 1.0 merge.1
  83.9 6.5 %collective-permute-done.29.refs_1_ = bf16[48,1664]{1,0:T(8,128)(2,1)S(1)} collective-permute-done((bf16[48,1664]{1,0:T(8,128)(2,1)S(1)}, bf16[48,1664]{1,0:T(8,128)(2,1)S(1)}, u32[]{:S(2)}, u32[]{:S(2)}) %collective-permute-start.29) | collective-permute-done | bytes 159776 | tf_op jit(solution)/shard_map/ppermute | solution.py:722
  90.4 1.3 %collective-permute-start.33 = (bf16[48,1536]{1,0:T(8,128)(2,1)S(1)}, bf16[48,1536]{1,0:T(8,128)(2,1)S(1)}, u32[]{:S(2)}, u32[]{:S(2)}) collective-permute-start(bf16[48,1536]{1,0:T(8,128)(2,1)S(1)} %get-tuple-element.180.refs_4_.refs_0_.refs_13_), channel_id=1, source_target_pairs={{0,6},{2,4},{4,2},{6,0},{8,14},{10,12},{12,10},{14,8},{16,22},{18,... | collective-permute-start | bytes 442376 | tf_op jit(solution)/shard_map/ppermute | solution.py:722
  91.6 1.2 %collective-permute-start.32 = (bf16[48,1536]{1,0:T(8,128)(2,1)S(1)}, bf16[48,1536]{1,0:T(8,128)(2,1)S(1)}, u32[]{:S(2)}, u32[]{:S(2)}) collective-permute-start(bf16[48,1536]{1,0:T(8,128)(2,1)S(1)} %get-tuple-element.180.refs_4_.refs_0_.refs_13_), channel_id=1, source_target_pairs={{0,4},{2,6},{4,0},{6,2},{8,12},{10,14},{12,8},{14,10},{16,20},{18,... | collective-permute-start | bytes 442376 | tf_op jit(solution)/shard_map/ppermute | solution.py:722
  92.9 1.0 collective-permute-start.31
  93.9 1.0 collective-permute-done.35.refs_2_.refs_11_
  95.4 2.7 %collective-permute-done.33.refs_3_.refs_16_ = bf16[48,1536]{1,0:T(8,128)(2,1)S(1)} collective-permute-done((bf16[48,1536]{1,0:T(8,128)(2,1)S(1)}, bf16[48,1536]{1,0:T(8,128)(2,1)S(1)}, u32[]{:S(2)}, u32[]{:S(2)}) %collective-permute-start.33) | collective-permute-done | bytes 147488 | tf_op jit(solution)/shard_map/ppermute | solution.py:722
  98.2 1.4 %collective-permute-done.32.refs_2_.refs_15_ = bf16[48,1536]{1,0:T(8,128)(2,1)S(1)} collective-permute-done((bf16[48,1536]{1,0:T(8,128)(2,1)S(1)}, bf16[48,1536]{1,0:T(8,128)(2,1)S(1)}, u32[]{:S(2)}, u32[]{:S(2)}) %collective-permute-start.32) | collective-permute-done | bytes 147488 | tf_op jit(solution)/shard_map/ppermute | solution.py:722
  99.9 1.2 %collective-permute-done.37.refs_1_ = f32[8,128]{1,0:T(8,128)S(1)} collective-permute-done((f32[8,128]{1,0:T(8,128)S(1)}, f32[8,128]{1,0:T(8,128)S(1)}, u32[]{:S(2)}, u32[]{:S(2)}) %collective-permute-start.37) | collective-permute-done | bytes 4128 | tf_op jit(solution)/shard_map/ppermute | solution.py:722
  101.0 5.8 %adamw.1 = (f32[192,4608]{1,0:T(8,128)}, f32[192,4608]{1,0:T(8,128)}, f32[192,4608]{1,0:T(8,128)}, bf16[192,4608]{1,0:T(8,128)(2,1)}, f32[6,384]{1,0:T(8,128)}, ...) custom-call(f32[8,128]{1,0:T(8,128)S(1)} %squares.3.refs_0_, f32[8,128]{1,0:T(8,128)S(1)} %collective-permute-done.37.refs_1_, ...), custom_call_target="tpu_custom_call" | custom-call | flops 4000000000 | bytes 23003136 | tf_op jit(solution)/shard_map/adamw/pallas_call | solution.py:1079
  (79 shorter events, 8.0 us)
Async XLA Ops:
  0.7 3.8 %copy-start.7 = (s32[8]{0:T(128)S(1)}, s32[8]{0:T(128)}, u32[]{:S(2)}) copy-start(s32[8]{0:T(128)} %param.15) | copy-start | bytes 100
  0.7 3.8 %copy-start.8 = (s32[8]{0:T(128)S(1)}, s32[8]{0:T(128)}, u32[]{:S(2)}) copy-start(s32[8]{0:T(128)} %param.14) | copy-start | bytes 100
  0.7 3.7 %copy-start.9 = (s32[8]{0:T(128)S(1)}, s32[8]{0:T(128)}, u32[]{:S(2)}) copy-start(s32[8]{0:T(128)} %param.13) | copy-start | bytes 100
  0.7 3.7 %copy-start.10 = (s32[1,16]{1,0:T(1,128)S(1)}, s32[1,16]{1,0:T(1,128)}, u32[]{:S(2)}) copy-start(s32[1,16]{1,0:T(1,128)} %param.12) | copy-start | bytes 196
  0.7 4.1 %copy-start.1 = (bf16[1024,384]{1,0:T(8,128)(2,1)S(1)}, bf16[1024,384]{1,0:T(8,128)(2,1)}, u32[]{:S(2)}) copy-start(bf16[1024,384]{1,0:T(8,128)(2,1)} %refs_0_.7) | copy-start | bytes 2359300
  2.9 2.0 %collective-permute-start = (bf16[192,1152]{1,0:T(8,128)(2,1)S(1)}, bf16[192,1152]{1,0:T(8,128)(2,1)S(1)}, u32[]{:S(2)}, u32[]{:S(2)}) collective-permute-start(bf16[192,1152]{1,0:T(8,128)(2,1)S(1)} %get-tuple-element.101.refs_2_), channel_id=1, source_target_pairs={{0,1},{1,0},{2,3},{3,2},{4,5},{5,4},{6,7},{7,6},{8,9},{9,8},{10,11... | collective-permute-start | bytes 1327112 | tf_op jit(solution)/shard_map/ppermute | solution.py:722
  3.4 1.4 %collective-permute-start.1 = (f32[6,384]{1,0:T(8,128)S(1)}, f32[6,384]{1,0:T(8,128)S(1)}, u32[]{:S(2)}, u32[]{:S(2)}) collective-permute-start(f32[6,384]{1,0:T(8,128)S(1)} %copy-done.4), channel_id=1, source_target_pairs={{0,1},{1,0},{2,3},{3,2},{4,5},{5,4},{6,7},{7,6},{8,9},{9,8},{10,11... | collective-permute-start | bytes 27656 | tf_op jit(solution)/shard_map/ppermute | solution.py:722
  3.5 6.4 %collective-permute-start.2 = (bf16[192,384]{1,0:T(8,128)(2,1)S(1)}, bf16[192,384]{1,0:T(8,128)(2,1)S(1)}, u32[]{:S(2)}, u32[]{:S(2)}) collective-permute-start(bf16[192,384]{1,0:T(8,128)(2,1)S(1)} %get-tuple-element.109.refs_5_), channel_id=1, source_target_pairs={{0,1},{1,0},{2,3},{3,2},{4,5},{5,4},{6,7},{7,6},{8,9},{9,8},{10,11... | collective-permute-start | bytes 442376 | tf_op jit(solution)/shard_map/ppermute | solution.py:722
  3.9 6.0 %collective-permute-start.3 = (bf16[192,1536]{1,0:T(8,128)(2,1)S(1)}, bf16[192,1536]{1,0:T(8,128)(2,1)S(1)}, u32[]{:S(2)}, u32[]{:S(2)}) collective-permute-start(bf16[192,1536]{1,0:T(8,128)(2,1)S(1)} %get-tuple-element.110.refs_7_), channel_id=1, source_target_pairs={{0,1},{1,0},{2,3},{3,2},{4,5},{5,4},{6,7},{7,6},{8,9},{9,8},{10,11... | collective-permute-start | bytes 1769480 | tf_op jit(solution)/shard_map/ppermute | solution.py:722
  4.0 6.0 %collective-permute-start.4 = (bf16[192,1536]{1,0:T(8,128)(2,1)S(1)}, bf16[192,1536]{1,0:T(8,128)(2,1)S(1)}, u32[]{:S(2)}, u32[]{:S(2)}) collective-permute-start(bf16[192,1536]{1,0:T(8,128)(2,1)S(1)} %get-tuple-element.111.refs_9_), channel_id=1, source_target_pairs={{0,1},{1,0},{2,3},{3,2},{4,5},{5,4},{6,7},{7,6},{8,9},{9,8},{10,11... | collective-permute-start | bytes 1769480 | tf_op jit(solution)/shard_map/ppermute | solution.py:722
  14.3 1.3 %collective-permute-start.5 = (f32[16,384]{1,0:T(8,128)S(1)}, f32[16,384]{1,0:T(8,128)S(1)}, u32[]{:S(2)}, u32[]{:S(2)}) collective-permute-start(f32[16,384]{1,0:T(8,128)S(1)} %get-tuple-element.112.refs_1_), channel_id=1, source_target_pairs={{0,1},{1,0},{2,3},{3,2},{4,5},{5,4},{6,7},{7,6},{8,9},{9,8},{10,11... | collective-permute-start | bytes 73736 | tf_op jit(solution)/shard_map/ppermute | solution.py:722
  15.6 7.2 %collective-permute-start.8 = (bf16[16,512]{1,0:T(8,128)(2,1)S(1)}, bf16[16,512]{1,0:T(8,128)(2,1)S(1)}, u32[]{:S(2)}, u32[]{:S(2)}) collective-permute-start(bf16[16,512]{1,0:T(8,128)(2,1)S(1)} %get-tuple-element.119.refs_1_.refs_0_.refs_6_), channel_id=1, source_target_pairs={{0,24},{2,26},{4,28},{6,30},{8,16},{10,18},{12,20},{14,22},{16,8},... | collective-permute-start | bytes 49160 | tf_op jit(solution)/shard_map/ppermute | solution.py:722
  20.5 4.6 %collective-permute-start.7 = (bf16[16,512]{1,0:T(8,128)(2,1)S(1)}, bf16[16,512]{1,0:T(8,128)(2,1)S(1)}, u32[]{:S(2)}, u32[]{:S(2)}) collective-permute-start(bf16[16,512]{1,0:T(8,128)(2,1)S(1)} %get-tuple-element.119.refs_1_.refs_0_.refs_6_), channel_id=1, source_target_pairs={{0,16},{2,18},{4,20},{6,22},{8,24},{10,26},{12,28},{14,30},{16,0},... | collective-permute-start | bytes 49160 | tf_op jit(solution)/shard_map/ppermute | solution.py:722
  20.5 4.6 %collective-permute-start.6 = (bf16[16,512]{1,0:T(8,128)(2,1)S(1)}, bf16[16,512]{1,0:T(8,128)(2,1)S(1)}, u32[]{:S(2)}, u32[]{:S(2)}) collective-permute-start(bf16[16,512]{1,0:T(8,128)(2,1)S(1)} %get-tuple-element.119.refs_1_.refs_0_.refs_6_), channel_id=1, source_target_pairs={{0,8},{2,10},{4,12},{6,14},{8,0},{10,2},{12,4},{14,6},{16,24},{18,... | collective-permute-start | bytes 49160 | tf_op jit(solution)/shard_map/ppermute | solution.py:722
  22.6 6.1 %copy-start = (f32[192,4608]{1,0:T(8,128)S(1)}, f32[192,4608]{1,0:T(8,128)}, u32[]{:S(2)}) copy-start(f32[192,4608]{1,0:T(8,128)} %refs_0_.4) | copy-start | bytes 10616836
  22.7 6.0 %copy-start.2 = (f32[192,4608]{1,0:T(8,128)S(1)}, f32[192,4608]{1,0:T(8,128)}, u32[]{:S(2)}) copy-start(f32[192,4608]{1,0:T(8,128)} %refs_1_.3) | copy-start | bytes 10616836
  22.7 6.0 %copy-start.3 = (f32[192,4608]{1,0:T(8,128)S(1)}, f32[192,4608]{1,0:T(8,128)}, u32[]{:S(2)}) copy-start(f32[192,4608]{1,0:T(8,128)} %refs_2_.3) | copy-start | bytes 10616836
  22.7 6.0 %copy-start.5 = (f32[6,384]{1,0:T(8,128)S(1)}, f32[6,384]{1,0:T(8,128)}, u32[]{:S(2)}) copy-start(f32[6,384]{1,0:T(8,128)} %refs_4_.3) | copy-start | bytes 27652
  22.7 6.0 %copy-start.6 = (f32[6,384]{1,0:T(8,128)S(1)}, f32[6,384]{1,0:T(8,128)}, u32[]{:S(2)}) copy-start(f32[6,384]{1,0:T(8,128)} %refs_5_.1) | copy-start | bytes 27652
  25.1 5.6 %collective-permute-start.11 = (bf16[4,16,512]{2,1,0:T(8,128)(2,1)S(1)}, bf16[4,16,512]{2,1,0:T(8,128)(2,1)S(1)}, u32[]{:S(2)}, u32[]{:S(2)}) collective-permute-start(bf16[4,16,512]{2,1,0:T(8,128)(2,1)S(1)} %join.1.refs_8_), channel_id=1, source_target_pairs={{0,6},{2,4},{4,2},{6,0},{8,14},{10,12},{12,10},{14,8},{16,22},{18,... | collective-permute-start | bytes 196616 | tf_op jit(solution)/shard_map/ppermute | solution.py:722
  27.6 4.3 %collective-permute-start.10 = (bf16[4,16,512]{2,1,0:T(8,128)(2,1)S(1)}, bf16[4,16,512]{2,1,0:T(8,128)(2,1)S(1)}, u32[]{:S(2)}, u32[]{:S(2)}) collective-permute-start(bf16[4,16,512]{2,1,0:T(8,128)(2,1)S(1)} %join.1.refs_8_), channel_id=1, source_target_pairs={{0,4},{2,6},{4,0},{6,2},{8,12},{10,14},{12,8},{14,10},{16,20},{18,... | collective-permute-start | bytes 196616 | tf_op jit(solution)/shard_map/ppermute | solution.py:722
  28.2 4.3 %collective-permute-start.9 = (bf16[4,16,512]{2,1,0:T(8,128)(2,1)S(1)}, bf16[4,16,512]{2,1,0:T(8,128)(2,1)S(1)}, u32[]{:S(2)}, u32[]{:S(2)}) collective-permute-start(bf16[4,16,512]{2,1,0:T(8,128)(2,1)S(1)} %join.1.refs_8_), channel_id=1, source_target_pairs={{0,2},{2,0},{4,6},{6,4},{8,10},{10,8},{12,14},{14,12},{16,18},{18,... | collective-permute-start | bytes 196616 | tf_op jit(solution)/shard_map/ppermute | solution.py:722
  35.7 3.0 %collective-permute-start.13 = (bf16[4,4,48,384]{3,2,1,0:T(8,128)(2,1)S(1)}, bf16[4,4,48,384]{3,2,1,0:T(8,128)(2,1)S(1)}, u32[]{:S(2)}, u32[]{:S(2)}) collective-permute-start(bf16[4,4,48,384]{3,2,1,0:T(8,128)(2,1)S(1)} %get-tuple-element.139), channel_id=1, source_target_pairs={{0,1},{1,0},{2,3},{3,2},{4,5},{5,4},{6,7},{7,6},{8,9},{9,8},{10,11... | collective-permute-start | bytes 1769480 | tf_op jit(solution)/shard_map/ppermute | solution.py:722
  38.1 2.2 %collective-permute-start.12 = (bf16[4,4,48,384]{3,2,1,0:T(8,128)(2,1)S(1)}, bf16[4,4,48,384]{3,2,1,0:T(8,128)(2,1)S(1)}, u32[]{:S(2)}, u32[]{:S(2)}) collective-permute-start(bf16[4,4,48,384]{3,2,1,0:T(8,128)(2,1)S(1)} %get-tuple-element.137), channel_id=1, source_target_pairs={{0,1},{1,0},{2,3},{3,2},{4,5},{5,4},{6,7},{7,6},{8,9},{9,8},{10,11... | collective-permute-start | bytes 1769480 | tf_op jit(solution)/shard_map/ppermute | solution.py:722
  40.4 10.0 %collective-permute-start.15 = (bf16[2,4,48,384]{3,2,1,0:T(8,128)(2,1)S(1)}, bf16[2,4,48,384]{3,2,1,0:T(8,128)(2,1)S(1)}, u32[]{:S(2)}, u32[]{:S(2)}) collective-permute-start(bf16[2,4,48,384]{3,2,1,0:T(8,128)(2,1)S(1)} %get-tuple-element.160), channel_id=1, source_target_pairs={{0,4},{2,6},{4,0},{6,2},{8,12},{10,14},{12,8},{14,10},{16,20},{18,... | collective-permute-start | bytes 884744 | tf_op jit(solution)/shard_map/ppermute | solution.py:722
  42.0 9.0 %collective-permute-start.14 = (bf16[2,4,48,384]{3,2,1,0:T(8,128)(2,1)S(1)}, bf16[2,4,48,384]{3,2,1,0:T(8,128)(2,1)S(1)}, u32[]{:S(2)}, u32[]{:S(2)}) collective-permute-start(bf16[2,4,48,384]{3,2,1,0:T(8,128)(2,1)S(1)} %get-tuple-element.159), channel_id=1, source_target_pairs={{0,2},{2,0},{4,6},{6,4},{8,10},{10,8},{12,14},{14,12},{16,18},{18,... | collective-permute-start | bytes 884744 | tf_op jit(solution)/shard_map/ppermute | solution.py:722
  51.2 6.6 %collective-permute-start.17 = (bf16[4,48,384]{2,1,0:T(8,128)(2,1)S(1)}, bf16[4,48,384]{2,1,0:T(8,128)(2,1)S(1)}, u32[]{:S(2)}, u32[]{:S(2)}) collective-permute-start(bf16[4,48,384]{2,1,0:T(8,128)(2,1)S(1)} %get-tuple-element.165), channel_id=1, source_target_pairs={{0,4},{2,6},{4,0},{6,2},{8,12},{10,14},{12,8},{14,10},{16,20},{18,... | collective-permute-start | bytes 442376 | tf_op jit(solution)/shard_map/ppermute | solution.py:722
  51.7 6.0 %collective-permute-start.18 = (bf16[4,48,384]{2,1,0:T(8,128)(2,1)S(1)}, bf16[4,48,384]{2,1,0:T(8,128)(2,1)S(1)}, u32[]{:S(2)}, u32[]{:S(2)}) collective-permute-start(bf16[4,48,384]{2,1,0:T(8,128)(2,1)S(1)} %get-tuple-element.167), channel_id=1, source_target_pairs={{0,2},{2,0},{4,6},{6,4},{8,10},{10,8},{12,14},{14,12},{16,18},{18,... | collective-permute-start | bytes 442376 | tf_op jit(solution)/shard_map/ppermute | solution.py:722
  56.2 6.0 %collective-permute-start.16 = (bf16[4,48,1664]{2,1,0:T(8,128)(2,1)S(1)}, bf16[4,48,1664]{2,1,0:T(8,128)(2,1)S(1)}, u32[]{:S(2)}, u32[]{:S(2)}) collective-permute-start(bf16[4,48,1664]{2,1,0:T(8,128)(2,1)S(1)} %get-tuple-element.164), channel_id=1, source_target_pairs={{0,1},{1,0},{2,3},{3,2},{4,5},{5,4},{6,7},{7,6},{8,9},{9,8},{10,11... | collective-permute-start | bytes 1916936 | tf_op jit(solution)/shard_map/ppermute | solution.py:722
  57.1 25.7 %collective-permute-start.30 = (bf16[576,384]{1,0:T(8,128)(2,1)S(1)}, bf16[576,384]{1,0:T(8,128)(2,1)S(1)}, u32[]{:S(2)}, u32[]{:S(2)}) collective-permute-start(bf16[576,384]{1,0:T(8,128)(2,1)S(1)} %input_backward.1.refs_4_.refs_0_), channel_id=1, source_target_pairs={{0,1},{1,0},{2,3},{3,2},{4,5},{5,4},{6,7},{7,6},{8,9},{9,8},{10,11... | collective-permute-start | bytes 1327112 | tf_op jit(solution)/shard_map/ppermute | solution.py:722
  57.8 5.8 %collective-permute-start.22 = (bf16[2,48,384]{2,1,0:T(8,128)(2,1)S(1)}, bf16[2,48,384]{2,1,0:T(8,128)(2,1)S(1)}, u32[]{:S(2)}, u32[]{:S(2)}) collective-permute-start(bf16[2,48,384]{2,1,0:T(8,128)(2,1)S(1)} %get-tuple-element.176), channel_id=1, source_target_pairs={{0,8},{2,10},{4,12},{6,14},{8,0},{10,2},{12,4},{14,6},{16,24},{18,... | collective-permute-start | bytes 221192 | tf_op jit(solution)/shard_map/ppermute | solution.py:722
  57.9 7.3 %collective-permute-start.23 = (bf16[2,48,384]{2,1,0:T(8,128)(2,1)S(1)}, bf16[2,48,384]{2,1,0:T(8,128)(2,1)S(1)}, u32[]{:S(2)}, u32[]{:S(2)}) collective-permute-start(bf16[2,48,384]{2,1,0:T(8,128)(2,1)S(1)} %get-tuple-element.177), channel_id=1, source_target_pairs={{0,16},{2,18},{4,20},{6,22},{8,24},{10,26},{12,28},{14,30},{16,0},... | collective-permute-start | bytes 221192 | tf_op jit(solution)/shard_map/ppermute | solution.py:722
  59.9 6.8 %collective-permute-start.24 = (bf16[2,48,384]{2,1,0:T(8,128)(2,1)S(1)}, bf16[2,48,384]{2,1,0:T(8,128)(2,1)S(1)}, u32[]{:S(2)}, u32[]{:S(2)}) collective-permute-start(bf16[2,48,384]{2,1,0:T(8,128)(2,1)S(1)} %get-tuple-element.178), channel_id=1, source_target_pairs={{0,24},{2,26},{4,28},{6,30},{8,16},{10,18},{12,20},{14,22},{16,8},... | collective-permute-start | bytes 221192 | tf_op jit(solution)/shard_map/ppermute | solution.py:722
  62.4 9.0 %collective-permute-start.19 = (bf16[48,1664]{1,0:T(8,128)(2,1)S(1)}, bf16[48,1664]{1,0:T(8,128)(2,1)S(1)}, u32[]{:S(2)}, u32[]{:S(2)}) collective-permute-start(bf16[48,1664]{1,0:T(8,128)(2,1)S(1)} %get-tuple-element.173), channel_id=1, source_target_pairs={{0,2},{2,0},{4,6},{6,4},{8,10},{10,8},{12,14},{14,12},{16,18},{18,... | collective-permute-start | bytes 479240 | tf_op jit(solution)/shard_map/ppermute | solution.py:722
  63.7 8.7 %collective-permute-start.20 = (bf16[48,1664]{1,0:T(8,128)(2,1)S(1)}, bf16[48,1664]{1,0:T(8,128)(2,1)S(1)}, u32[]{:S(2)}, u32[]{:S(2)}) collective-permute-start(bf16[48,1664]{1,0:T(8,128)(2,1)S(1)} %get-tuple-element.174), channel_id=1, source_target_pairs={{0,4},{2,6},{4,0},{6,2},{8,12},{10,14},{12,8},{14,10},{16,20},{18,... | collective-permute-start | bytes 479240 | tf_op jit(solution)/shard_map/ppermute | solution.py:722
  65.2 7.2 %collective-permute-start.21 = (bf16[48,1664]{1,0:T(8,128)(2,1)S(1)}, bf16[48,1664]{1,0:T(8,128)(2,1)S(1)}, u32[]{:S(2)}, u32[]{:S(2)}) collective-permute-start(bf16[48,1664]{1,0:T(8,128)(2,1)S(1)} %get-tuple-element.175), channel_id=1, source_target_pairs={{0,6},{2,4},{4,2},{6,0},{8,14},{10,12},{12,10},{14,8},{16,22},{18,... | collective-permute-start | bytes 479240 | tf_op jit(solution)/shard_map/ppermute | solution.py:722
  66.8 7.8 %collective-permute-start.28 = (bf16[2,48,384]{2,1,0:T(8,128)(2,1)S(1)}, bf16[2,48,384]{2,1,0:T(8,128)(2,1)S(1)}, u32[]{:S(2)}, u32[]{:S(2)}) collective-permute-start(bf16[2,48,384]{2,1,0:T(8,128)(2,1)S(1)} %low_plane_sum.2.refs_4_.refs_0_), channel_id=1, source_target_pairs={{0,24},{2,26},{4,28},{6,30},{8,16},{10,18},{12,20},{14,22},{16,8},... | collective-permute-start | bytes 221192 | tf_op jit(solution)/shard_map/ppermute | solution.py:722
  71.4 5.9 %collective-permute-start.27 = (bf16[2,48,384]{2,1,0:T(8,128)(2,1)S(1)}, bf16[2,48,384]{2,1,0:T(8,128)(2,1)S(1)}, u32[]{:S(2)}, u32[]{:S(2)}) collective-permute-start(bf16[2,48,384]{2,1,0:T(8,128)(2,1)S(1)} %low_plane_sum.2.refs_4_.refs_0_), channel_id=1, source_target_pairs={{0,16},{2,18},{4,20},{6,22},{8,24},{10,26},{12,28},{14,30},{16,0},... | collective-permute-start | bytes 221192 | tf_op jit(solution)/shard_map/ppermute | solution.py:722
  72.3 6.4 %collective-permute-start.26 = (bf16[2,48,384]{2,1,0:T(8,128)(2,1)S(1)}, bf16[2,48,384]{2,1,0:T(8,128)(2,1)S(1)}, u32[]{:S(2)}, u32[]{:S(2)}) collective-permute-start(bf16[2,48,384]{2,1,0:T(8,128)(2,1)S(1)} %low_plane_sum.2.refs_4_.refs_0_), channel_id=1, source_target_pairs={{0,8},{2,10},{4,12},{6,14},{8,0},{10,2},{12,4},{14,6},{16,24},{18,... | collective-permute-start | bytes 221192 | tf_op jit(solution)/shard_map/ppermute | solution.py:722
  72.4 9.9 %collective-permute-start.25 = (bf16[48,1664]{1,0:T(8,128)(2,1)S(1)}, bf16[48,1664]{1,0:T(8,128)(2,1)S(1)}, u32[]{:S(2)}, u32[]{:S(2)}) collective-permute-start(bf16[48,1664]{1,0:T(8,128)(2,1)S(1)} %low_plane_sum.3.refs_4_.refs_0_), channel_id=1, source_target_pairs={{0,8},{2,10},{4,12},{6,14},{8,0},{10,2},{12,4},{14,6},{16,24},{18,... | collective-permute-start | bytes 479240 | tf_op jit(solution)/shard_map/ppermute | solution.py:722
  78.8 14.1 %collective-permute-start.36 = (bf16[8,48,384]{2,1,0:T(8,128)(2,1)S(1)}, bf16[8,48,384]{2,1,0:T(8,128)(2,1)S(1)}, u32[]{:S(2)}, u32[]{:S(2)}) collective-permute-start(bf16[8,48,384]{2,1,0:T(8,128)(2,1)S(1)} %chain.1.refs_2_.refs_0_.refs_9_), channel_id=1, source_target_pairs={{0,6},{2,4},{4,2},{6,0},{8,14},{10,12},{12,10},{14,8},{16,22},{18,... | collective-permute-start | bytes 884744 | tf_op jit(solution)/shard_map/ppermute | solution.py:722
  80.0 14.9 %collective-permute-start.35 = (bf16[8,48,384]{2,1,0:T(8,128)(2,1)S(1)}, bf16[8,48,384]{2,1,0:T(8,128)(2,1)S(1)}, u32[]{:S(2)}, u32[]{:S(2)}) collective-permute-start(bf16[8,48,384]{2,1,0:T(8,128)(2,1)S(1)} %chain.1.refs_2_.refs_0_.refs_9_), channel_id=1, source_target_pairs={{0,4},{2,6},{4,0},{6,2},{8,12},{10,14},{12,8},{14,10},{16,20},{18,... | collective-permute-start | bytes 884744 | tf_op jit(solution)/shard_map/ppermute | solution.py:722
  81.2 14.1 %collective-permute-start.34 = (bf16[8,48,384]{2,1,0:T(8,128)(2,1)S(1)}, bf16[8,48,384]{2,1,0:T(8,128)(2,1)S(1)}, u32[]{:S(2)}, u32[]{:S(2)}) collective-permute-start(bf16[8,48,384]{2,1,0:T(8,128)(2,1)S(1)} %chain.1.refs_2_.refs_0_.refs_9_), channel_id=1, source_target_pairs={{0,2},{2,0},{4,6},{6,4},{8,10},{10,8},{12,14},{14,12},{16,18},{18,... | collective-permute-start | bytes 884744 | tf_op jit(solution)/shard_map/ppermute | solution.py:722
  82.4 8.0 %collective-permute-start.29 = (bf16[48,1664]{1,0:T(8,128)(2,1)S(1)}, bf16[48,1664]{1,0:T(8,128)(2,1)S(1)}, u32[]{:S(2)}, u32[]{:S(2)}) collective-permute-start(bf16[48,1664]{1,0:T(8,128)(2,1)S(1)} %low_next.1.refs_2_.refs_0_), channel_id=1, source_target_pairs={{0,16},{2,18},{4,20},{6,22},{8,24},{10,26},{12,28},{14,30},{16,0},... | collective-permute-start | bytes 479240 | tf_op jit(solution)/shard_map/ppermute | solution.py:722
  90.4 7.8 %collective-permute-start.33 = (bf16[48,1536]{1,0:T(8,128)(2,1)S(1)}, bf16[48,1536]{1,0:T(8,128)(2,1)S(1)}, u32[]{:S(2)}, u32[]{:S(2)}) collective-permute-start(bf16[48,1536]{1,0:T(8,128)(2,1)S(1)} %get-tuple-element.180.refs_4_.refs_0_.refs_13_), channel_id=1, source_target_pairs={{0,6},{2,4},{4,2},{6,0},{8,14},{10,12},{12,10},{14,8},{16,22},{18,... | collective-permute-start | bytes 442376 | tf_op jit(solution)/shard_map/ppermute | solution.py:722
  91.6 7.9 %collective-permute-start.32 = (bf16[48,1536]{1,0:T(8,128)(2,1)S(1)}, bf16[48,1536]{1,0:T(8,128)(2,1)S(1)}, u32[]{:S(2)}, u32[]{:S(2)}) collective-permute-start(bf16[48,1536]{1,0:T(8,128)(2,1)S(1)} %get-tuple-element.180.refs_4_.refs_0_.refs_13_), channel_id=1, source_target_pairs={{0,4},{2,6},{4,0},{6,2},{8,12},{10,14},{12,8},{14,10},{16,20},{18,... | collective-permute-start | bytes 442376 | tf_op jit(solution)/shard_map/ppermute | solution.py:722
  92.9 6.8 %collective-permute-start.31 = (bf16[48,1536]{1,0:T(8,128)(2,1)S(1)}, bf16[48,1536]{1,0:T(8,128)(2,1)S(1)}, u32[]{:S(2)}, u32[]{:S(2)}) collective-permute-start(bf16[48,1536]{1,0:T(8,128)(2,1)S(1)} %get-tuple-element.180.refs_4_.refs_0_.refs_13_), channel_id=1, source_target_pairs={{0,2},{2,0},{4,6},{6,4},{8,10},{10,8},{12,14},{14,12},{16,18},{18,... | collective-permute-start | bytes 442376 | tf_op jit(solution)/shard_map/ppermute | solution.py:722
  99.8 1.2 %collective-permute-start.37 = (f32[8,128]{1,0:T(8,128)S(1)}, f32[8,128]{1,0:T(8,128)S(1)}, u32[]{:S(2)}, u32[]{:S(2)}) collective-permute-start(f32[8,128]{1,0:T(8,128)S(1)} %squares.3.refs_0_), channel_id=1, source_target_pairs={{0,1},{1,0},{2,3},{3,2},{4,5},{5,4},{6,7},{7,6},{8,9},{9,8},{10,11... | collective-permute-start | bytes 12296 | tf_op jit(solution)/shard_map/ppermute | solution.py:722
  (1 other events, 2.7 us)
